TPU v7x, 512 devices: a whole 4x8x8 slice. The times are simulated.
512 devices in a mesh: ctx: 32 (over x_hi, y, core), ch: 16 (over x_lo, z).
Axes of the slice: x: 4 (x_hi: 2, x_lo: 2; x = x_hi * 2 + x_lo), y: 8, z: 8, core: 2. Of those that a mesh axis runs over, the one named last changes fastest.
Arguments:
- signal: bfloat16 [65536, 2048], P('ctx', 'ch'), may hold values from -6 to 6
- cond_in: bfloat16 [2048, 64], P('ch'), may hold values from -0.125 to 0.125
- cond_bias: float32 [64], replicated, may hold values from -4 to 4
- cond_out: bfloat16 [64, 2048], P(None, 'ch'), may hold values from -0.75 to 0.75
- skip_gain: float32 [2048], P('ch'), may hold values from 0.5 to 1.5
Outputs:
- mixed: bfloat16 [65536, 2048], P('ctx', 'ch')
All inputs are finite; a program needn't handle non-finite values.
Results may differ from a plain program's by a relative error of at most 0.00125.
Values may be sent and summed in bfloat16 or wider, within the bound.
No kernel may reach another device: no remote copies, remote signals or barrier semaphores. Data moves between devices by JAX's collectives and lax.ppermute only.
A program may use at most 64 MiB of HBM per device.

v0:
```python
import math

import jax
import jax.numpy as jnp
from jax import lax
from jax.sharding import PartitionSpec as P

exact_mode = lax.Precision.HIGHEST


def pick_factor(length):
    chosen = 1
    for candidate in range(1, math.isqrt(length) + 1):
        if length % candidate == 0:
            chosen = candidate
    return chosen


def dft_table(length, direction):
    counter = jnp.arange(length, dtype=jnp.int32)
    residue = counter[:, None] * counter[None, :] % length
    phases = 2.0 * math.pi / length * residue.astype(jnp.float32)
    return (jnp.cos(phases), direction * jnp.sin(phases))


def twiddle(first_index, second_index, modulus, direction):
    residue = first_index[:, None] * second_index[None, :] % modulus
    phases = 2.0 * math.pi / modulus * residue.astype(jnp.float32)
    return (jnp.cos(phases)[:, :, None], (direction * jnp.sin(phases))[:, :, None])


def rotate(real_part, imag_part, cosine, sine):
    return (real_part * cosine - imag_part * sine, real_part * sine + imag_part * cosine)


def lead_transform(table, real_part, imag_part):
    table_re, table_im = table
    leading = real_part.shape[0]
    flat_re = real_part.reshape(leading, -1)
    flat_im = imag_part.reshape(leading, -1)
    out_re = jnp.dot(table_re, flat_re, precision=exact_mode) - jnp.dot(
        table_im, flat_im, precision=exact_mode
    )
    out_im = jnp.dot(table_re, flat_im, precision=exact_mode) + jnp.dot(
        table_im, flat_re, precision=exact_mode
    )
    return (out_re.reshape(real_part.shape), out_im.reshape(imag_part.shape))


def middle_transform(table, real_part, imag_part):
    table_re, table_im = table

    def contract(matrix, values):
        return jnp.einsum("kj,ajc->akc", matrix, values, precision=exact_mode)

    out_re = contract(table_re, real_part) - contract(table_im, imag_part)
    out_im = contract(table_re, imag_part) + contract(table_im, real_part)
    return (out_re, out_im)


def condition(feature, cond_in, cond_bias, cond_out):
    weight_in = cond_in.astype(jnp.float32)
    partial_sum = jnp.dot(feature, weight_in, precision=exact_mode)
    pre = lax.psum(partial_sum, "ch")
    hidden = jax.nn.gelu(pre + cond_bias, approximate=False)
    return jnp.dot(hidden, cond_out.astype(jnp.float32), precision=exact_mode)


def on_device(signal, cond_in, cond_bias, cond_out, skip_gain):
    members = lax.axis_size("ctx")
    position = lax.axis_index("ctx")
    seq_local, chan_local = signal.shape
    blocks = seq_local // members
    total_len = seq_local * members
    first_radix = pick_factor(seq_local)
    second_radix = seq_local // first_radix
    first_count = jnp.arange(first_radix, dtype=jnp.int32)
    second_count = jnp.arange(second_radix, dtype=jnp.int32)
    pieces = lax.all_to_all(
        signal.reshape(members, blocks, chan_local), "ctx", split_axis=0, concat_axis=0, tiled=True
    )
    table_fwd = dft_table(members, -1.0)
    flat = pieces.astype(jnp.float32).reshape(members, -1)
    part_re = jnp.dot(table_fwd[0], flat, precision=exact_mode).reshape(members, blocks, chan_local)
    part_im = jnp.dot(table_fwd[1], flat, precision=exact_mode).reshape(members, blocks, chan_local)
    offsets = position * blocks + jnp.arange(blocks, dtype=jnp.int32)
    cosine, sine = twiddle(jnp.arange(members, dtype=jnp.int32), offsets, total_len, -1.0)
    part_re, part_im = rotate(part_re, part_im, cosine, sine)
    column_re, column_im = (
        lax.all_to_all(part_re, "ctx", split_axis=0, concat_axis=1, tiled=True),
        lax.all_to_all(part_im, "ctx", split_axis=0, concat_axis=1, tiled=True),
    )
    column_re = column_re.reshape(first_radix, second_radix, chan_local)
    column_im = column_im.reshape(first_radix, second_radix, chan_local)
    spec_re, spec_im = lead_transform(dft_table(first_radix, -1.0), column_re, column_im)
    cosine, sine = twiddle(first_count, second_count, seq_local, -1.0)
    spec_re, spec_im = rotate(spec_re, spec_im, cosine, sine)
    spec_re, spec_im = middle_transform(dft_table(second_radix, -1.0), spec_re, spec_im)
    spec_re = spec_re.reshape(seq_local, chan_local)
    spec_im = spec_im.reshape(seq_local, chan_local)
    feature = jnp.log1p((spec_re * spec_re + spec_im * spec_im) / total_len)
    spectral_gain = condition(feature, cond_in, cond_bias, cond_out)
    prod_re = spec_re * spectral_gain
    prod_im = spec_im * spectral_gain
    work_re, work_im = (prod_re, prod_im)
    width_now = work_re.shape[1]
    work_re = work_re.reshape(first_radix, second_radix, width_now)
    work_im = work_im.reshape(first_radix, second_radix, width_now)
    work_re, work_im = middle_transform(dft_table(second_radix, 1.0), work_re, work_im)
    cosine, sine = twiddle(first_count, second_count, seq_local, 1.0)
    work_re, work_im = rotate(work_re, work_im, cosine, sine)
    work_re, work_im = lead_transform(dft_table(first_radix, 1.0), work_re, work_im)
    work_re = work_re.reshape(seq_local, width_now)
    work_im = work_im.reshape(seq_local, width_now)
    cosine, sine = twiddle(
        jnp.arange(seq_local, dtype=jnp.int32), jnp.reshape(position, (1,)), total_len, 1.0
    )
    work_re, work_im = rotate(
        work_re, work_im, cosine.reshape(seq_local, 1), sine.reshape(seq_local, 1)
    )
    work_re = work_re.reshape(members, blocks, width_now)
    work_im = work_im.reshape(members, blocks, width_now)
    table_back = dft_table(members, 1.0)
    rows_re, rows_im = (
        lax.all_to_all(work_re, "ctx", split_axis=0, concat_axis=0, tiled=True),
        lax.all_to_all(work_im, "ctx", split_axis=0, concat_axis=0, tiled=True),
    )
    flat_re = rows_re.reshape(members, -1)
    flat_im = rows_im.reshape(members, -1)
    real_out = jnp.dot(table_back[0], flat_re, precision=exact_mode) - jnp.dot(
        table_back[1], flat_im, precision=exact_mode
    )
    response = real_out.reshape(members, blocks, chan_local)
    response = response / total_len
    returned = lax.all_to_all(response, "ctx", split_axis=0, concat_axis=0, tiled=True)
    combined = returned.reshape(seq_local, chan_local) + skip_gain[None, :] * signal.astype(
        jnp.float32
    )
    return combined.astype(jnp.bfloat16)


def solution(mesh):
    return jax.shard_map(
        on_device,
        mesh=mesh,
        in_specs=(P("ctx", "ch"), P("ch", None), P(), P(None, "ch"), P("ch")),
        out_specs=P("ctx", "ch"),
        check_vma=False,
    )
```

profile of v0, /device:TPU:1, one launch (start us, length us, event | category | flops | bytes accessed | tf_op | source)
XLA Modules:
  0.0 395.3 jit_solution(4785847297843551521)
XLA Ops:
  6.5 0.0 copy-start
  6.5 11.4 %all-to-all-start = ((bf16[32,64,128]{2,1,0:T(8,128)(2,1)}), bf16[32,64,128]{2,1,0:T(8,128)(2,1)S(1)}, u32[]{:S(2)}, u32[]{:S(2)}) async-start(bf16[32,64,128]{2,1,0:T(8,128)(2,1)} %bitcast.176), calls=%async_computation | async-start | bytes 1048576 | tf_op jit(solution)/shard_map/all_to_all | solution.py:79
  17.9 0.1 fusion.201
  18.0 0.1 copy.33
  18.1 0.1 copy.35
  18.2 17.8 %all-to-all-done = bf16[32,64,128]{2,1,0:T(8,128)(2,1)S(1)} async-done(((bf16[32,64,128]{2,1,0:T(8,128)(2,1)}), bf16[32,64,128]{2,1,0:T(8,128)(2,1)S(1)}, u32[]{:S(2)}, u32[]{:S(2)}) %all-to-all-start) | async-done | bytes 524320 | tf_op jit(solution)/shard_map/all_to_all | solution.py:79
  36.0 0.8 fusion.45
  36.7 1.1 multiply_subtract_fusion.1
  37.9 1.6 copy.36
  39.5 5.7 %all-to-all-start.1 = ((f32[32,64,128]{2,1,0:T(8,128)}), f32[32,64,128]{2,1,0:T(8,128)S(1)}, u32[]{:S(2)}, u32[]{:S(2)}) async-start(f32[32,64,128]{2,1,0:T(8,128)} %copy.36), calls=%async_computation.1 | async-start | bytes 2097152 | tf_op jit(solution)/shard_map/all_to_all | solution.py:90
  45.2 1.6 copy.37
  46.8 26.3 %all-to-all-done.1 = f32[32,64,128]{2,1,0:T(8,128)S(1)} async-done(((f32[32,64,128]{2,1,0:T(8,128)}), f32[32,64,128]{2,1,0:T(8,128)S(1)}, u32[]{:S(2)}, u32[]{:S(2)}) %all-to-all-start.1) | async-done | bytes 1048608 | tf_op jit(solution)/shard_map/all_to_all | solution.py:90
  73.1 6.2 %all-to-all-start.2 = ((f32[32,64,128]{2,1,0:T(8,128)}), f32[32,64,128]{2,1,0:T(8,128)S(1)}, u32[]{:S(2)}, u32[]{:S(2)}) async-start(f32[32,64,128]{2,1,0:T(8,128)} %copy.37), calls=%async_computation.2 | async-start | bytes 2097152 | tf_op jit(solution)/shard_map/all_to_all | solution.py:91
  79.2 0.3 all-reduce.2.cloned.1.call-start
  79.6 0.1 broadcast_multiply_fusion
  79.7 1.6 fusion.25
  81.3 25.7 %all-to-all-done.2 = f32[32,64,128]{2,1,0:T(8,128)S(1)} async-done(((f32[32,64,128]{2,1,0:T(8,128)}), f32[32,64,128]{2,1,0:T(8,128)S(1)}, u32[]{:S(2)}, u32[]{:S(2)}) %all-to-all-start.2) | async-done | bytes 1048608 | tf_op jit(solution)/shard_map/all_to_all | solution.py:91
  107.0 1.6 fusion.21
  108.6 1.6 fusion.1
  110.2 0.2 copy.42
  110.4 1.6 fusion.2
  112.0 0.2 copy.43
  112.2 1.4 fusion.19
  113.6 1.1 fusion.147
  114.8 1.2 fusion.149
  115.9 1.2 convolution_add_fusion.3
  117.1 1.2 convolution_subtract_fusion.4
  118.3 0.0 copy-start.2
  118.3 0.4 fusion.30
  118.8 0.3 copy-done.2
  119.0 1.5 fusion.331
  120.5 0.0 all-reduce.2.cloned.1.call-update
  120.6 0.1 fusion.199
  120.6 0.0 copy-start.4
  120.7 0.1 fusion.194
  120.8 131.6 %all-reduce.2.cloned.1.call-done = f32[2048,64]{0,1:T(8,128)} async-done(((f32[2048,64]{0,1:T(8,128)}), f32[2048,64]{0,1:T(8,128)}) %all-reduce.2.cloned.1.call-update) | async-done | bytes 524304 | tf_op jit(solution)/shard_map/psum | solution.py:64
  252.3 0.0 copy-done
  252.3 0.0 copy-done.4
  252.3 3.2 bitcast_multiply_fusion.10
  255.5 1.1 fusion.145
  256.7 1.2 fusion.143
  257.8 1.2 convolution_subtract_fusion.3
  259.1 1.9 multiply_subtract_fusion
  260.9 1.6 fusion.17
  262.5 1.6 fusion.13
  264.1 1.6 fusion.3
  265.7 0.2 copy.46
  265.9 1.6 fusion.4
  267.5 0.2 copy.47
  267.7 1.6 fusion.12
  269.4 48.0 %all_to_all.38 = f32[32,64,128]{2,1,0:T(8,128)S(1)} all-to-all(f32[32,64,128]{2,1,0:T(8,128)S(1)} %get-tuple-element.8), channel_id=1, replica_groups=mesh['ctx'=32,'ch'=16] {'ctx'}, dimensions={0} | all-to-all | bytes 2097152 | tf_op jit(solution)/shard_map/all_to_all | solution.py:125
  317.4 6.5 %all-to-all-start.4 = ((f32[32,64,128]{2,1,0:T(8,128)}), f32[32,64,128]{2,1,0:T(8,128)S(1)}, u32[]{:S(2)}, u32[]{:S(2)}) async-start(f32[32,64,128]{2,1,0:T(8,128)} %get-tuple-element.7), calls=%async_computation.4 | async-start | bytes 2097152 | tf_op jit(solution)/shard_map/all_to_all | solution.py:126
  323.9 1.6 fusion.8
  325.5 26.0 %all-to-all-done.4 = f32[32,64,128]{2,1,0:T(8,128)S(1)} async-done(((f32[32,64,128]{2,1,0:T(8,128)}), f32[32,64,128]{2,1,0:T(8,128)S(1)}, u32[]{:S(2)}, u32[]{:S(2)}) %all-to-all-start.4) | async-done | bytes 1048608 | tf_op jit(solution)/shard_map/all_to_all | solution.py:126
  351.6 1.6 fusion.5
  353.2 0.2 copy.50
  353.4 0.0 copy-start.1
  353.4 0.0 copy-start.3
  353.4 33.9 %all_to_all.39 = f32[32,64,128]{2,1,0:T(8,128)S(1)} all-to-all(f32[32,64,128]{2,1,0:T(8,128)S(1)} %bitcast.175), channel_id=1, replica_groups=mesh['ctx'=32,'ch'=16] {'ctx'}, dimensions={0} | all-to-all | bytes 2097152 | tf_op jit(solution)/shard_map/all_to_all | solution.py:135
  387.3 0.0 copy-done.1
  387.3 0.0 copy-done.3
  387.3 0.9 fusion.27
  (1 shorter events, 0.0 us)
Async XLA Ops:
  6.5 245.8 %copy-start = (bf16[64,128]{1,0:T(8,128)(2,1)S(1)}, bf16[64,128]{1,0:T(8,128)(2,1)}, u32[]{:S(2)}) copy-start(bf16[64,128]{1,0:T(8,128)(2,1)} %param.8) | copy-start | bytes 49156
  6.5 29.4 %all-to-all-start = ((bf16[32,64,128]{2,1,0:T(8,128)(2,1)}), bf16[32,64,128]{2,1,0:T(8,128)(2,1)S(1)}, u32[]{:S(2)}, u32[]{:S(2)}) async-start(bf16[32,64,128]{2,1,0:T(8,128)(2,1)} %bitcast.176), calls=%async_computation | async-start | bytes 1048576 | tf_op jit(solution)/shard_map/all_to_all | solution.py:79
  39.5 33.6 %all-to-all-start.1 = ((f32[32,64,128]{2,1,0:T(8,128)}), f32[32,64,128]{2,1,0:T(8,128)S(1)}, u32[]{:S(2)}, u32[]{:S(2)}) async-start(f32[32,64,128]{2,1,0:T(8,128)} %copy.36), calls=%async_computation.1 | async-start | bytes 2097152 | tf_op jit(solution)/shard_map/all_to_all | solution.py:90
  73.1 33.9 %all-to-all-start.2 = ((f32[32,64,128]{2,1,0:T(8,128)}), f32[32,64,128]{2,1,0:T(8,128)S(1)}, u32[]{:S(2)}, u32[]{:S(2)}) async-start(f32[32,64,128]{2,1,0:T(8,128)} %copy.37), calls=%async_computation.2 | async-start | bytes 2097152 | tf_op jit(solution)/shard_map/all_to_all | solution.py:91
  79.2 173.1 %all-reduce.2.cloned.1.call-start = ((), (), s32[]{:S(2)}) async-start(), calls=%async_computation.6 | async-start | bytes 1048576 | tf_op jit(solution)/shard_map/psum | solution.py:64
  118.3 0.7 copy-start.2
  120.6 131.7 %copy-start.4 = (f32[64]{0:T(128)S(1)}, f32[64]{0:T(128)}, u32[]{:S(2)}) copy-start(f32[64]{0:T(128)} %param.7) | copy-start | bytes 772
  317.4 34.2 %all-to-all-start.4 = ((f32[32,64,128]{2,1,0:T(8,128)}), f32[32,64,128]{2,1,0:T(8,128)S(1)}, u32[]{:S(2)}, u32[]{:S(2)}) async-start(f32[32,64,128]{2,1,0:T(8,128)} %get-tuple-element.7), calls=%async_computation.4 | async-start | bytes 2097152 | tf_op jit(solution)/shard_map/all_to_all | solution.py:126
  353.4 33.9 %copy-start.1 = (bf16[2048,128]{1,0:T(8,128)(2,1)S(1)}, bf16[2048,128]{1,0:T(8,128)(2,1)}, u32[]{:S(2)}) copy-start(bf16[2048,128]{1,0:T(8,128)(2,1)} %param.5) | copy-start | bytes 1572868
  353.4 33.9 %copy-start.3 = (f32[128]{0:T(128)S(1)}, f32[128]{0:T(128)}, u32[]{:S(2)}) copy-start(f32[128]{0:T(128)} %param.9) | copy-start | bytes 1540
Sparse Core Ops, SparseCore 0:
  120.7 131.5 all-reduce.1
where the time goes:
time: 402 us; the launch traced here: 395 us
  waiting for transfers between devices  227 us (56%)
  blocking collectives  81.9 us (20%)
  matrix products  32.6 us (8%)
  starting transfers between devices  30.1 us (7%)
  between operations  13.9 us (3%)
  other arithmetic  4.77 us (1%)
  local copies, waits for them, and re-layouts  4.57 us (1%)
    psum x1, waiting for transfers between devices, condition(): pre = lax.psum(partial_sum, 'ch')  132 us
    all_to_all x1, blocking collectives, on_device(): lax.all_to_all(work_re, 'ctx', split_axis=0, concat_axis=0, tiled=True)  48 us
    all_to_all x1, blocking collectives, on_device(): lax.all_to_all(response, 'ctx', split_axis=0, concat_axis=0, tiled=True)  33.9 us
    all_to_all x1, waiting for transfers between devices, on_device(): lax.all_to_all(part_re, 'ctx', split_axis=0, concat_axis=1, tiled=True)  26.3 us
    all_to_all x1, waiting for transfers between devices, on_device(): lax.all_to_all(work_im, 'ctx', split_axis=0, concat_axis=0, tiled=True)  26 us
    all_to_all x1, waiting for transfers between devices, on_device(): lax.all_to_all(part_im, 'ctx', split_axis=0, concat_axis=1, tiled=True)  25.7 us
    all_to_all x1, waiting for transfers between devices, on_device(): lax.all_to_all(signal.reshape(members, blocks, chan_local), 'ctx', split_...  17.8 us
    all_to_all x1, starting transfers between devices, on_device(): lax.all_to_all(signal.reshape(members, blocks, chan_local), 'ctx', split_...  11.4 us
  transfers between devices with their start and end apart: 5, of which 5 were waited for; matrix products, arithmetic and copies ran while one was open for 1% of the time, Pallas kernels for 0%

commit v1 on v0

v1 whole, which is shorter than its diff:
```python
import functools
import math

import jax
import jax.numpy as jnp
import numpy as np
from jax import lax
from jax.experimental import pallas as pl
from jax.experimental.pallas import tpu as pltpu
from jax.sharding import PartitionSpec as P

f32, bf16, f16 = jnp.float32, jnp.bfloat16, jnp.float16

RADIX = 256
HALF = RADIX // 2
SEQ = RADIX * RADIX
GAIN_SCALE = 0.25


def split_const(values):
    high = values.astype(np.float32).astype(jnp.bfloat16)
    low = (values - high.astype(np.float64)).astype(np.float32).astype(jnp.bfloat16)
    return high, low


@functools.lru_cache(maxsize=None)
def tables():
    n = np.arange(RADIX, dtype=np.float64)
    k = np.arange(HALF, dtype=np.float64)
    tau = 2.0 * np.pi
    angle = tau * np.outer(k, n) / RADIX
    first = np.concatenate([np.cos(angle), -np.sin(angle)], 0)
    first[HALF] = np.cos(math.pi * n)
    first = np.concatenate(split_const(first), 0)
    angle = tau * np.outer(k, n) / SEQ
    cos_f, sin_f = np.cos(angle), np.sin(angle)
    cos_g = cos_f.copy()
    cos_g[0] = 0.0
    shared = tau * n * (HALF + SEQ // 2) / SEQ
    twf = np.stack([cos_f, sin_f, cos_g]).astype(np.float32)
    row0 = np.zeros((3, 8, RADIX))
    row0[0, 0], row0[1, 0] = np.cos(shared), np.sin(shared)
    row0[2, :] = np.cos(math.pi * n)
    row0 = row0.astype(np.float32)
    angle = tau * np.outer(n, n) / RADIX
    wre, wim = np.cos(angle), -np.sin(angle)
    full = [np.concatenate([wre, -wim], 1), np.concatenate([wim, wre], 1)]
    second = np.stack([np.concatenate([f[:HALF] for f in full], 0),
                       np.concatenate([f[HALF:] for f in full], 0)])
    second = np.stack(split_const(second))
    vre, vim = np.cos(angle), np.sin(angle)
    inv = np.stack([
        np.concatenate([np.concatenate([vre[:, s], -vim[:, s]], 1),
                        np.concatenate([vim[:, s], vre[:, s]], 1)], 0)
        for s in (slice(0, HALF), slice(HALF, RADIX))])
    inv = np.stack(split_const(inv))
    angle = tau * np.outer(n, k) / SEQ
    twi = np.stack([np.cos(angle), np.sin(angle),
                    np.repeat(np.cos(shared)[:, None], HALF, 1),
                    np.repeat(np.sin(shared)[:, None], HALF, 1)]).astype(np.float32)
    angle = tau * np.outer(n, k) / RADIX
    last = np.concatenate([np.cos(angle), -np.sin(angle)], 1)
    last[:, HALF] = np.cos(math.pi * n)
    last = np.stack(split_const(last * (2.0 / SEQ)))
    return dict(first=first, twf=twf, row0=row0, second=second, inv=inv, twi=twi, last=last)


def split(x):
    high = x.astype(bf16)
    return high, (x - high.astype(f32)).astype(bf16)


def mm(a, b):
    return jnp.dot(a, b, preferred_element_type=f32)


def nt(a, b):
    return lax.dot_general(a, b, (((1,), (1,)), ((), ())), preferred_element_type=f32)


def iota(shape, axis):
    return lax.broadcasted_iota(jnp.int32, shape, axis)


def pack_kernel(x_ref, out_ref, left, right):
    rows = x_ref.shape[0] // RADIX
    chan = x_ref.shape[1]
    for a in range(rows):
        block = x_ref[RADIX * a : RADIX * (a + 1), :].astype(f32).T
        left[pl.ds(a, chan, stride=rows), :] = block[:, :128]
        right[pl.ds(a, chan, stride=rows), :] = block[:, 128:]
    out_ref[:, :, :128] = left[...].astype(bf16).reshape(out_ref.shape[:2] + (128,))
    out_ref[:, :, 128:] = right[...].astype(bf16).reshape(out_ref.shape[:2] + (128,))


def unpack_kernel(r_ref, out_ref, left, right):
    rows = out_ref.shape[0] // RADIX
    chan = out_ref.shape[1]
    left[...] = r_ref[:, :, :128].astype(f32).reshape(left.shape)
    right[...] = r_ref[:, :, 128:].astype(f32).reshape(right.shape)
    for a in range(rows):
        out_ref[RADIX * a : RADIX * a + 128, :] = (
            left[pl.ds(a, chan, stride=rows), :].T.astype(bf16))
        out_ref[RADIX * a + 128 : RADIX * (a + 1), :] = (
            right[pl.ds(a, chan, stride=rows), :].T.astype(bf16))


def weights_kernel(members, per, rows, cin_ref, cout_ref, win_ref, wout_ref):
    chan, hid = cin_ref.shape
    big = per * members * rows
    lane = iota((chan, big), 1)
    pick = per * ((lane // rows) % members) + lane // (members * rows)
    rep = (iota((chan, big), 0) == pick).astype(f32).astype(bf16)
    spread = lax.dot_general(cin_ref[...], rep, (((0,), (0,)), ((), ())),
                             preferred_element_type=f32)
    lane = iota((hid, big), 1) % rows
    for k in range(rows):
        win_ref[k * hid : (k + 1) * hid, :] = jnp.where(lane == k, spread, 0.0).astype(bf16)
    wide = rows * hid
    copy = (iota((hid, wide), 1) % hid == iota((hid, wide), 0)).astype(f32).astype(bf16)
    columns = mm(jnp.transpose(cout_ref[...].astype(f32)).astype(bf16), copy)
    spread = lax.dot_general(rep, columns.astype(bf16), (((0,), (0,)), ((), ())),
                             preferred_element_type=f32)
    keep = iota((big, wide), 0) % rows == iota((big, wide), 1) // hid
    wout_ref[...] = jnp.where(keep, spread, 0.0).astype(bf16)


def forward_kernel(per, rows, r_ref, first_ref, twf_ref, row0_ref, second_ref,
                   feat_ref, spec_ref, nyq_ref, hi, lo, hi2, lo2):
    members = r_ref.shape[0]
    values = r_ref[...].astype(f32)
    first_row = iota((8, RADIX), 0) == 0
    spare = jnp.zeros((8, 128), f32)
    feat_spare = jnp.zeros((8, 128), f32)
    spare_lane = iota((8, 128), 1)
    for c in range(per):
        x = values[:, rows * c : rows * (c + 1), :].reshape(RADIX, RADIX).astype(bf16)
        a = mm(first_ref[...], x)
        a = a[:RADIX] + a[RADIX:]
        re, im = a[:HALF], a[HALF:]
        out_re = re * twf_ref[0] + im * twf_ref[1]
        out_im = im * twf_ref[2] - re * twf_ref[1]
        place = pl.ds(HALF * c, HALF)
        for at, part in ((0, out_re), (RADIX, out_im)):
            high, low = split(part)
            hi[place, at : at + RADIX], lo[place, at : at + RADIX] = high, low
            hi2[place, at : at + RADIX], lo2[place, at : at + RADIX] = high, low
        lead = im[0:8]
        top = pl.ds(HALF * c, 16)
        alt_re = jnp.concatenate(
            [jnp.where(first_row, lead * row0_ref[0], out_re[0:8]), out_re[8:16]], 0)
        alt_im = jnp.concatenate(
            [jnp.where(first_row, -lead * row0_ref[1], out_im[0:8]), out_im[8:16]], 0)
        for at, part in ((0, alt_re), (RADIX, alt_im)):
            high, low = split(part)
            hi2[top, at : at + RADIX], lo2[top, at : at + RADIX] = high, low
        nyq = jnp.sum(re[0:1] * row0_ref[2, 0:1], axis=1, keepdims=True)
        spare = jnp.where(spare_lane == c, nyq, spare)
    feat_spare = jnp.log1p(spare * spare * (1.0 / SEQ))
    nyq_ref[...] = spare
    width = HALF * per
    feat_ref[:, :, width:] = jnp.broadcast_to(feat_spare[None], (members, rows, 128))
    for part, (h, l) in enumerate(((hi, lo), (hi2, lo2))):
        s = (nt(second_ref[0, part], h[...]) + nt(second_ref[0, part], l[...])
             + nt(second_ref[1, part], h[...]))
        spec_ref[part] = s
        re, im = s[:HALF], s[HALF:]
        feature = jnp.log1p((re * re + im * im) * (1.0 / SEQ))
        count = HALF // rows
        feat_ref[part * count : (part + 1) * count, :, :width] = feature.reshape(
            count, rows, width)


def reduce_kernel(per, rows, hid, f_ref, win_ref, out_ref):
    members = f_ref.shape[0]
    groups = out_ref.shape[0]
    chunk = members * rows
    f = f_ref[...].reshape(chunk, f_ref.shape[2])
    stack = jnp.concatenate([f[:, HALF * c : HALF * (c + 1)] for c in range(per)], 0)
    high, low = split(stack)
    pre = mm(win_ref[...], jnp.concatenate([high, low], 1))
    pre = pre[:, :HALF] + pre[:, HALF:]
    main = pre.shape[0] // groups
    out_ref[:, :main, :] = pre.reshape(groups, main, HALF)
    last = f[:, HALF * per :]
    lane = iota(last.shape, 1)
    stack = jnp.concatenate([jnp.where(lane == c, last, 0.0) for c in range(per)], 0)
    high, low = split(stack)
    extra = mm(win_ref[:hid], jnp.concatenate([high, low], 1))
    extra = jnp.sum(extra, axis=1, keepdims=True)
    extra = jnp.sum(jnp.where(iota((hid, 128), 0) == iota((hid, 128), 1), extra, 0.0),
                    axis=0, keepdims=True)
    out_ref[:, main:, :] = jnp.broadcast_to(extra[None], (groups, 8, 128))


def gelu(v):
    return 0.5 * v * (1.0 + lax.erf(v * math.sqrt(0.5)))


def hidden_kernel(main, hid, r_ref, bias_ref, cout_ref, out_ref, gain_ref):
    groups = r_ref.shape[0]
    total = r_ref[0]
    for g in range(1, groups):
        total = total + r_ref[g]
    start = (lax.axis_index("ch") * main) % hid
    bias = bias_ref[...]
    column = jnp.sum(
        jnp.where(iota((main, hid), 1) == (iota((main, hid), 0) + start) % hid, bias, 0.0),
        axis=1, keepdims=True)
    hidden = gelu(total[:main] + column)
    out_ref[...] = jnp.broadcast_to(hidden[None], out_ref.shape)
    spare = gelu(total[main:, :hid] + bias)
    high, low = split(spare)
    gain_ref[...] = mm(high, cout_ref[...]) + mm(low, cout_ref[...])


def gain_kernel(per, rows, h_ref, wout_ref, out_ref):
    hidden = h_ref[...].reshape(wout_ref.shape[1], HALF)
    high, low = split(hidden)
    g = mm(wout_ref[...], jnp.concatenate([high, low], 1))
    g = (g[:, :HALF] + g[:, HALF:]) * GAIN_SCALE
    chunk = g.shape[0] // per
    members = out_ref.shape[0]
    for c in range(per):
        out_ref[:, :, HALF * c : HALF * (c + 1)] = g[chunk * c : chunk * (c + 1)].reshape(
            members, rows, HALF)


def inverse_kernel(per, rows, g_ref, spec_ref, nyq_ref, gain_ref, skip_ref, r_ref,
                   inv_ref, twi_ref, last_ref, row0_ref, out_ref):
    members = g_ref.shape[0]
    width = HALF * per
    count = members // 2
    sums = []
    for part in range(2):
        g = g_ref[part * count : (part + 1) * count].reshape(HALF, width)
        g = g * (1.0 / GAIN_SCALE)
        if part == 0:
            dc = (iota((HALF, width), 0) == 0) & (iota((HALF, width), 1) % HALF == 0)
            g = jnp.where(dc, 0.5 * g, g)
        s = spec_ref[part]
        high, low = split(jnp.concatenate([s[:HALF] * g, s[HALF:] * g], 0))
        sums.append(mm(inv_ref[0, part], high) + mm(inv_ref[0, part], low)
                    + mm(inv_ref[1, part], high))
    own = lax.axis_index("ctx") * per
    lane = iota((1, 128), 1)
    lane0 = iota((RADIX, HALF), 1) == 0
    pieces = []
    for c in range(per):
        cols = slice(HALF * c, HALF * (c + 1))
        top_re, top_im = sums[0][:RADIX, cols], sums[0][RADIX:, cols]
        bot_re, bot_im = sums[1][:RADIX, cols], sums[1][RADIX:, cols]
        re = jnp.where(lane0, top_re, top_re + bot_re)
        im = top_im + bot_im
        out_re = jnp.where(lane0, re, re * twi_ref[0] - im * twi_ref[1])
        out_im = jnp.where(lane0, bot_re * twi_ref[2] - bot_im * twi_ref[3],
                           re * twi_ref[1] + im * twi_ref[0])
        high, low = split(jnp.concatenate([out_re, out_im], 1))
        y = nt(last_ref[0], high) + nt(last_ref[0], low) + nt(last_ref[1], high)
        mine = lane == own + c
        skip = jnp.sum(jnp.where(mine, skip_ref[...], 0.0), axis=1, keepdims=True)
        gain = jnp.sum(jnp.where(mine, gain_ref[0:1], 0.0), axis=1, keepdims=True)
        spare = jnp.sum(jnp.where(lane == c, nyq_ref[0:1], 0.0), axis=1, keepdims=True)
        x = r_ref[:, rows * c : rows * (c + 1), :].astype(f32).reshape(RADIX, RADIX)
        y = y + (spare * gain * (1.0 / SEQ)) * row0_ref[2, 0:1] + skip * x
        pieces.append(y.reshape(members, rows, RADIX))
    out_ref[...] = jnp.concatenate(pieces, 1).astype(bf16)


def call(kernel, outs, scratch=(), flops=0, interpret=False):
    vmem = pl.BlockSpec(memory_space=pltpu.VMEM)
    many = isinstance(outs, (list, tuple))

    def run(*args):
        return pl.pallas_call(
            kernel,
            out_shape=outs,
            in_specs=[vmem] * len(args),
            out_specs=[vmem] * len(outs) if many else vmem,
            scratch_shapes=list(scratch),
            compiler_params=pltpu.CompilerParams(vmem_limit_bytes=40 * 1024 * 1024),
        )(*args)

    return run


def exchange(x, axis):
    return lax.all_to_all(x, axis, split_axis=0, concat_axis=0, tiled=True)


def on_device(signal, cond_in, cond_bias, cond_out, skip_gain):
    shape = jax.ShapeDtypeStruct
    members = lax.axis_size("ctx")
    groups = lax.axis_size("ch")
    seq_local, chan = signal.shape
    hid = cond_in.shape[1]
    per = chan // members
    rows = seq_local // RADIX
    width = HALF * per
    t = {name: jnp.asarray(value) for name, value in tables().items()}
    halves = [pltpu.VMEM((chan * rows, 128), f32)] * 2
    piece = shape((members, per * rows, RADIX), bf16)

    packed = call(pack_kernel, piece, halves)(signal)
    received = exchange(packed, "ctx")
    big = per * members * rows
    win, wout = call(functools.partial(weights_kernel, members, per, rows),
                     [shape((rows * hid, big), bf16), shape((big, rows * hid), bf16)])(
                         cond_in, cond_out)
    feat, spec, nyq = call(
        functools.partial(forward_kernel, per, rows),
        [shape((members, rows, width + 128), f32), shape((2, RADIX, width), f32),
         shape((8, 128), f32)],
        [pltpu.VMEM((width, 2 * RADIX), bf16)] * 4)(
            received, t["first"], t["twf"], t["row0"], t["second"])
    feat = exchange(feat.astype(f16), "ctx").astype(f32)
    main = rows * hid // groups
    partial = call(functools.partial(reduce_kernel, per, rows, hid),
                   shape((groups, main + 8, HALF), f32))(feat, win)
    partial = exchange(partial, "ch")
    hidden, spare_gain = call(functools.partial(hidden_kernel, main, hid),
                              [shape((groups, main, HALF), f32), shape((8, chan), f32)])(
                                  partial, cond_bias.reshape(1, hid), cond_out)
    hidden = exchange(hidden, "ch")
    gain = call(functools.partial(gain_kernel, per, rows),
                shape((members, rows, width), f32))(hidden, wout)
    gain = exchange(gain.astype(f16), "ctx").astype(f32)
    mixed = call(functools.partial(inverse_kernel, per, rows), piece)(
        gain, spec, nyq, spare_gain, skip_gain.reshape(1, chan), received,
        t["inv"], t["twi"], t["last"], t["row0"])
    mixed = exchange(mixed, "ctx")
    return call(unpack_kernel, shape((seq_local, chan), bf16), halves)(mixed)


def solution(mesh):
    return jax.shard_map(
        on_device,
        mesh=mesh,
        in_specs=(P("ctx", "ch"), P("ch", None), P(), P(None, "ch"), P("ch")),
        out_specs=P("ctx", "ch"),
        check_vma=False,
    )
```

time: 402 us -> 138 us (0.34); the launches traced: 395 us -> 137 us
  waiting for transfers between devices: 227 us -> 12.1 us
  matrix products: 32.6 us -> 0 us
  starting transfers between devices: 30.1 us -> 5.77 us
  blocking collectives: 81.9 us -> 106 us
  between operations: 13.9 us -> 0.17 us
  Pallas kernels: 0 us -> 6.75 us
    psum x1 -> x0, waiting for transfers between devices: 132 us -> none  [condition(): pre = lax.psum(partial_sum, 'ch')]
    all_to_all x4 -> x1, waiting for transfers between devices: 95.8 us -> 12.1 us  [exchange(): return lax.all_to_all(x, axis, split_axis=0, concat_axis=0, tiled=True)]
    dot_general x22 -> x0, matrix products: 32.6 us -> none  [the longest x8 10 us: contract(): return jnp.einsum('kj,ajc->akc', matrix, values, precision=exact_mode)]
    all_to_all x4 -> x1, starting transfers between devices: 29.8 us -> 5.77 us  [exchange(): return lax.all_to_all(x, axis, split_axis=0, concat_axis=0, tiled=True)]
    all_to_all x2 -> x5, blocking collectives: 81.9 us -> 106 us  [exchange(): return lax.all_to_all(x, axis, split_axis=0, concat_axis=0, tiled=True)]
    pallas_call x0 -> x8, Pallas kernels: none -> 6.75 us  [run(): pl.pallas_call(kernel, out_shape=outs, in_specs=[vmem] * len(args), out_s...]
    unnamed x15 -> x29, local copies, waits for them, and re-layouts: 1.22 us -> 5.75 us
  transfers between devices with their start and end apart: 5 -> 1, of which waited for: 5 -> 1; matrix products, arithmetic and copies ran while one was open for 1% -> 0% of each run, Pallas kernels for 0% -> 1%
where the time goes in v1:
time: 138 us; the launch traced here: 137 us
  blocking collectives  106 us (77%)
  waiting for transfers between devices  12.1 us (9%)
  Pallas kernels  6.75 us (5%)
  starting transfers between devices  5.77 us (4%)
  local copies, waits for them, and re-layouts  5.75 us (4%)
    all_to_all x5, blocking collectives, exchange(): return lax.all_to_all(x, axis, split_axis=0, concat_axis=0, tiled=True)  106 us
    all_to_all x1, waiting for transfers between devices, exchange(): return lax.all_to_all(x, axis, split_axis=0, concat_axis=0, tiled=True)  12.1 us
    pallas_call x8, Pallas kernels, run(): pl.pallas_call(kernel, out_shape=outs, in_specs=[vmem] * len(args), out_s...  6.75 us
    all_to_all x1, starting transfers between devices, exchange(): return lax.all_to_all(x, axis, split_axis=0, concat_axis=0, tiled=True)  5.77 us
    unnamed x29, local copies, waits for them, and re-layouts  5.75 us
  transfers between devices with their start and end apart: 1, of which 1 were waited for; matrix products, arithmetic and copies ran while one was open for 0% of the time, Pallas kernels for 1%

profile of v1, /device:TPU:1, one launch (start us, length us, event | category | flops | bytes accessed | tf_op | source)
XLA Modules:
  0.0 137.3 jit_solution(2373082564343962317)
XLA Ops:
  0.0 0.0 copy-start.1
  0.0 0.0 copy-start.5
  0.0 1.1 copy-done.5
  1.1 0.3 shard_map.118
  1.4 0.0 copy-start.6
  1.5 0.0 copy-start.8
  1.5 0.0 copy-start.9
  1.5 29.2 %all_to_all.30.r_ref = bf16[32,32,256]{2,1,0:T(8,128)(2,1)S(1)} all-to-all(bf16[32,32,256]{2,1,0:T(8,128)(2,1)S(1)} %shard_map.118), channel_id=1, replica_groups=mesh['ctx'=32,'ch'=16] {'ctx'}, dimensions={0} | all-to-all | bytes 1048576 | tf_op jit(solution)/shard_map/all_to_all | solution.py:288
  30.7 0.0 copy-done.1
  30.7 0.0 copy-done.6
  30.7 0.0 copy-done.8
  30.7 0.0 copy-done.9
  30.7 1.6 %shard_map.119 = (f32[32,8,640]{2,1,0:T(8,128)S(1)}, f32[2,256,512]{2,1,0:T(8,128)S(1)}, f32[8,128]{1,0:T(8,128)S(1)}) custom-call(bf16[32,32,256]{2,1,0:T(8,128)(2,1)S(1)} %all_to_all.30.r_ref, bf16[512,256]{1,0:T(8,128)(2,1)S(1)} %copy-done.8, f32[3,128,256]{2,1,0:T(8,128)S(1)} %copy-done.6, f32[3,8,256]{2,1,0:T(8,128)S(1)} %copy-done.9, ...), custom_call_target="tpu_custom_call" | custom-call | tf_op jit(solution)/shard_map/pallas_call | solution.py:275
  32.3 0.8 convert_element_type.12
  33.1 0.0 copy-start.13
  33.1 5.8 %all-to-all-start.1 = ((f16[32,8,640]{2,1,0:T(8,128)(2,1)}), f16[32,8,640]{2,1,0:T(8,128)(2,1)S(1)}, u32[]{:S(2)}, u32[]{:S(2)}) async-start(f16[32,8,640]{2,1,0:T(8,128)(2,1)} %convert_element_type.12), calls=%async_computation.1 | async-start | bytes 655360 | tf_op jit(solution)/shard_map/all_to_all | solution.py:288
  38.8 0.0 copy-done.13
  38.8 0.0 copy-start.10
  38.9 0.1 copy.13.cin_ref
  39.0 0.6 copy-done.10
  39.6 0.8 shard_map.120
  40.3 0.0 copy-start.2
  40.4 1.0 copy-done.2
  41.3 12.1 %all-to-all-done.1 = f16[32,8,640]{2,1,0:T(8,128)(2,1)S(1)} async-done(((f16[32,8,640]{2,1,0:T(8,128)(2,1)}), f16[32,8,640]{2,1,0:T(8,128)(2,1)S(1)}, u32[]{:S(2)}, u32[]{:S(2)}) %all-to-all-start.1) | async-done | bytes 327712 | tf_op jit(solution)/shard_map/all_to_all | solution.py:288
  53.5 0.0 copy-start.3
  53.5 1.2 copy-done.3
  54.7 0.6 shard_map.121
  55.3 18.0 %all_to_all.31.r_ref = f32[16,40,128]{2,1,0:T(8,128)S(1)} all-to-all(f32[16,40,128]{2,1,0:T(8,128)S(1)} %shard_map.121), channel_id=1, replica_groups=mesh['ctx'=32,'ch'=16] {'ch'}, dimensions={0} | all-to-all | bytes 655360 | tf_op jit(solution)/shard_map/all_to_all | solution.py:288
  73.4 0.0 copy-start.11
  73.4 0.7 copy-done.11
  74.0 0.1 shard_map.122
  74.2 14.5 %all_to_all.32.h_ref = f32[16,32,128]{2,1,0:T(8,128)S(1)} all-to-all(f32[16,32,128]{2,1,0:T(8,128)S(1)} %get-tuple-element.14), channel_id=1, replica_groups=mesh['ctx'=32,'ch'=16] {'ch'}, dimensions={0} | all-to-all | bytes 524288 | tf_op jit(solution)/shard_map/all_to_all | solution.py:288
  88.6 0.4 shard_map.123
  89.1 0.0 copy-start
  89.1 21.7 %all_to_all.33 = f16[32,8,512]{2,1,0:T(8,128)(2,1)S(1)} all-to-all(f16[32,8,512]{2,1,0:T(8,128)(2,1)S(1)} %convert_element_type.14), channel_id=1, replica_groups=mesh['ctx'=32,'ch'=16] {'ctx'}, dimensions={0} | all-to-all | bytes 524288 | tf_op jit(solution)/shard_map/all_to_all | solution.py:288
  110.9 0.0 copy-start.4
  110.9 0.0 copy-start.7
  110.9 0.1 convert_element_type.15.g_ref
  110.9 0.0 copy-start.12
  110.9 0.0 copy-done
  110.9 1.0 copy-done.4
  111.9 0.1 copy-done.7
  112.0 0.0 copy-done.12
  112.0 1.9 %shard_map.124 = bf16[32,32,256]{2,1,0:T(8,128)(2,1)S(1)} custom-call(f32[32,8,512]{2,1,0:T(8,128)S(1)} %convert_element_type.15.g_ref, f32[2,256,512]{2,1,0:T(8,128)S(1)} %get-tuple-element.16.spec_ref, f32[8,128]{1,0:T(8,128)S(1)} %get-tuple-element.17.nyq_ref, f32[8,128]{1,0:T(8,128)S(1)} %get-tuple-element.18.gain_ref, f32[1,128]{1,0:T(1,128)S(1)} %bitcast.3, ...), custom_call_target="tpu_custom_call" | custom-call | tf_op jit(solution)/shard_map/pallas_call | solution.py:275
  113.9 22.4 %all_to_all.34.r_ref = bf16[32,32,256]{2,1,0:T(8,128)(2,1)S(1)} all-to-all(bf16[32,32,256]{2,1,0:T(8,128)(2,1)S(1)} %shard_map.124), channel_id=1, replica_groups=mesh['ctx'=32,'ch'=16] {'ctx'}, dimensions={0} | all-to-all | bytes 1048576 | tf_op jit(solution)/shard_map/all_to_all | solution.py:288
  136.2 1.1 shard_map.125
  (2 shorter events, 0.1 us)
Async XLA Ops:
  0.0 30.7 %copy-start.1 = (bf16[2,2,256,512]{3,2,1,0:T(8,128)(2,1)S(1)}, bf16[2,2,256,512]{3,2,1,0:T(8,128)(2,1)}, u32[]{:S(2)}) copy-start(bf16[2,2,256,512]{3,2,1,0:T(8,128)(2,1)} %constant.17.clone.second_ref) | copy-start | bytes 3145732
  0.0 1.1 copy-start.5
  1.4 29.3 %copy-start.6 = (f32[3,128,256]{2,1,0:T(8,128)S(1)}, f32[3,128,256]{2,1,0:T(8,128)}, u32[]{:S(2)}) copy-start(f32[3,128,256]{2,1,0:T(8,128)} %constant.15.clone.twf_ref) | copy-start | bytes 1179652
  1.5 29.3 %copy-start.8 = (bf16[512,256]{1,0:T(8,128)(2,1)S(1)}, bf16[512,256]{1,0:T(8,128)(2,1)}, u32[]{:S(2)}) copy-start(bf16[512,256]{1,0:T(8,128)(2,1)} %constant.14.clone.first_ref) | copy-start | bytes 786436
  1.5 29.2 %copy-start.9 = (f32[3,8,256]{2,1,0:T(8,128)S(1)}, f32[3,8,256]{2,1,0:T(8,128)}, u32[]{:S(2)}) copy-start(f32[3,8,256]{2,1,0:T(8,128)} %constant.16.clone.row0_ref) | copy-start | bytes 73732
  33.1 5.8 %copy-start.13 = (bf16[128,64]{0,1:T(8,128)(2,1)S(1)}, bf16[128,64]{0,1:T(8,128)(2,1)}, u32[]{:S(2)}) copy-start(bf16[128,64]{0,1:T(8,128)(2,1)} %param.13) | copy-start | bytes 49156
  33.1 20.4 %all-to-all-start.1 = ((f16[32,8,640]{2,1,0:T(8,128)(2,1)}), f16[32,8,640]{2,1,0:T(8,128)(2,1)S(1)}, u32[]{:S(2)}, u32[]{:S(2)}) async-start(f16[32,8,640]{2,1,0:T(8,128)(2,1)} %convert_element_type.12), calls=%async_computation.1 | async-start | bytes 655360 | tf_op jit(solution)/shard_map/all_to_all | solution.py:288
  38.8 0.7 copy-start.10
  40.3 1.0 copy-start.2
  53.5 1.2 copy-start.3
  73.4 0.7 copy-start.11
  89.1 21.8 %copy-start = (bf16[2,2,512,256]{3,2,1,0:T(8,128)(2,1)S(1)}, bf16[2,2,512,256]{3,2,1,0:T(8,128)(2,1)}, u32[]{:S(2)}) copy-start(bf16[2,2,512,256]{3,2,1,0:T(8,128)(2,1)} %constant.18.clone.inv_ref) | copy-start | bytes 3145732
  110.9 1.0 copy-start.4
  110.9 1.1 copy-start.7
  110.9 1.0 copy-start.12

commit v2 on v1

v2 whole, which is shorter than its diff:
```python
import functools
import math

import jax
import jax.numpy as jnp
import numpy as np
from jax import lax
from jax.experimental import pallas as pl
from jax.experimental.pallas import tpu as pltpu
from jax.sharding import Mesh
from jax.sharding import PartitionSpec as P

f32, bf16, f16 = jnp.float32, jnp.bfloat16, jnp.float16

RADIX = 256
HALF = RADIX // 2
SEQ = RADIX * RADIX
GAIN_SCALE = 0.25
IN_SCALE = 2.0**18
OUT_SCALE = 2.0**16


def split_const(values):
    high = values.astype(np.float32).astype(jnp.bfloat16)
    low = (values - high.astype(np.float64)).astype(np.float32).astype(jnp.bfloat16)
    return high, low


@functools.lru_cache(maxsize=None)
def tables():
    n = np.arange(RADIX, dtype=np.float64)
    k = np.arange(HALF, dtype=np.float64)
    tau = 2.0 * np.pi
    angle = tau * np.outer(k, n) / RADIX
    first = np.concatenate([np.cos(angle), -np.sin(angle)], 0)
    first[HALF] = np.cos(math.pi * n)
    first = np.concatenate(split_const(first), 0)
    angle = tau * np.outer(k, n) / SEQ
    cos_f, sin_f = np.cos(angle), np.sin(angle)
    cos_g = cos_f.copy()
    cos_g[0] = 0.0
    shared = tau * n * (HALF + SEQ // 2) / SEQ
    twf = np.stack([cos_f, sin_f, cos_g]).astype(np.float32)
    row0 = np.zeros((3, 8, RADIX))
    row0[0, 0], row0[1, 0] = np.cos(shared), np.sin(shared)
    row0[2, :] = np.cos(math.pi * n)
    row0 = row0.astype(np.float32)
    angle = tau * np.outer(n, n) / RADIX
    wre, wim = np.cos(angle), -np.sin(angle)
    full = [np.concatenate([wre, -wim], 1), np.concatenate([wim, wre], 1)]
    second = np.stack([np.concatenate([f[:HALF] for f in full], 0),
                       np.concatenate([f[HALF:] for f in full], 0)])
    second = np.stack(split_const(second))
    vre, vim = np.cos(angle), np.sin(angle)
    inv = np.stack([
        np.concatenate([np.concatenate([vre[:, s], -vim[:, s]], 1),
                        np.concatenate([vim[:, s], vre[:, s]], 1)], 0)
        for s in (slice(0, HALF), slice(HALF, RADIX))])
    inv = np.stack(split_const(inv))
    angle = tau * np.outer(n, k) / RADIX
    last = np.concatenate([np.cos(angle), -np.sin(angle)], 1)
    last[:, HALF] = np.cos(math.pi * n)
    last = np.stack(split_const(last * (2.0 / SEQ)))
    return dict(first=first, twf=twf, row0=row0, second=second, inv=inv, last=last)


def split(x):
    high = x.astype(bf16)
    return high, (x - high.astype(f32)).astype(bf16)


def mm(a, b):
    return jnp.dot(a, b, preferred_element_type=f32)


def nt(a, b):
    return lax.dot_general(a, b, (((1,), (1,)), ((), ())), preferred_element_type=f32)


def iota(shape, axis):
    return lax.broadcasted_iota(jnp.int32, shape, axis)


def pack_kernel(x_ref, out_ref, left, right):
    rows = x_ref.shape[0] // RADIX
    chan = x_ref.shape[1]
    for a in range(rows):
        block = x_ref[RADIX * a : RADIX * (a + 1), :].astype(f32).T
        left[pl.ds(a, chan, stride=rows), :] = block[:, :128]
        right[pl.ds(a, chan, stride=rows), :] = block[:, 128:]
    out_ref[:, :, :128] = left[...].astype(bf16).reshape(out_ref.shape[:2] + (128,))
    out_ref[:, :, 128:] = right[...].astype(bf16).reshape(out_ref.shape[:2] + (128,))


def unpack_kernel(r_ref, out_ref, left, right):
    rows = out_ref.shape[0] // RADIX
    chan = out_ref.shape[1]
    left[...] = r_ref[:, :, :128].astype(f32).reshape(left.shape)
    right[...] = r_ref[:, :, 128:].astype(f32).reshape(right.shape)
    for a in range(rows):
        out_ref[RADIX * a : RADIX * a + 128, :] = (
            left[pl.ds(a, chan, stride=rows), :].T.astype(bf16))
        out_ref[RADIX * a + 128 : RADIX * (a + 1), :] = (
            right[pl.ds(a, chan, stride=rows), :].T.astype(bf16))


def forward_kernel(per, rows, block, r_ref, first_ref, twf_ref, row0_ref, second_ref, last_in_ref,
                   cin_ref, cout_in_ref, bias_in_ref, skip_in_ref,
                   feat_ref, spec_ref, nyq_ref, last_ref, cout_ref, bias_ref, skip_ref,
                   hi, lo, hi2, lo2):
    last_ref[...] = last_in_ref[...]
    cout_ref[...] = cout_in_ref[...]
    bias_ref[...] = jnp.broadcast_to(bias_in_ref[...], bias_ref.shape)
    skip_ref[...] = jnp.broadcast_to(skip_in_ref[...], skip_ref.shape)
    pieces = feat_ref.shape[0]
    values = r_ref[...].astype(f32)
    first_row = iota((8, RADIX), 0) == 0
    spare = jnp.zeros((8, 128), f32)
    spare_lane = iota((8, 128), 1)
    for c in range(per):
        x = values[:, block * c : block * (c + 1), :].reshape(RADIX, RADIX).astype(bf16)
        a = mm(first_ref[...], x)
        a = a[:RADIX] + a[RADIX:]
        re, im = a[:HALF], a[HALF:]
        out_re = re * twf_ref[0] + im * twf_ref[1]
        out_im = im * twf_ref[2] - re * twf_ref[1]
        place = pl.ds(HALF * c, HALF)
        for at, part in ((0, out_re), (RADIX, out_im)):
            high, low = split(part)
            hi[place, at : at + RADIX], lo[place, at : at + RADIX] = high, low
            hi2[place, at : at + RADIX], lo2[place, at : at + RADIX] = high, low
        lead = im[0:8]
        top = pl.ds(HALF * c, 16)
        alt_re = jnp.concatenate(
            [jnp.where(first_row, lead * row0_ref[0], out_re[0:8]), out_re[8:16]], 0)
        alt_im = jnp.concatenate(
            [jnp.where(first_row, -lead * row0_ref[1], out_im[0:8]), out_im[8:16]], 0)
        for at, part in ((0, alt_re), (RADIX, alt_im)):
            high, low = split(part)
            hi2[top, at : at + RADIX], lo2[top, at : at + RADIX] = high, low
        nyq = jnp.sum(re[0:1] * row0_ref[2, 0:1], axis=1, keepdims=True)
        spare = jnp.where(spare_lane == c, nyq, spare)
    nyq_ref[...] = spare
    chan = cin_ref.shape[1]
    own = (lax.axis_index("chip") * lax.axis_size("core") + lax.axis_index("core")) * per
    row = iota((8, chan), 0)
    select = ((iota((8, chan), 1) == own + row) & (row < per)).astype(f32).astype(bf16)
    tile = jnp.concatenate([nt(select, cin_ref[...]) * IN_SCALE,
                            nt(select, cout_in_ref[...]) * OUT_SCALE], 1)
    tile = jnp.where(iota((8, 128), 0) == per, jnp.log1p(spare * spare * (1.0 / SEQ)), tile)
    width = HALF * per
    feat_ref[:, :, width:] = jnp.broadcast_to(tile[None], (pieces, rows, 128))
    for part, (h, l) in enumerate(((hi, lo), (hi2, lo2))):
        s = (nt(second_ref[0, part], h[...]) + nt(second_ref[0, part], l[...])
             + nt(second_ref[1, part], h[...]))
        spec_ref[part] = s
        re, im = s[:HALF], s[HALF:]
        feature = jnp.log1p((re * re + im * im) * (1.0 / SEQ))
        count = HALF // rows
        feat_ref[part * count : (part + 1) * count, :, :width] = feature.reshape(
            count, rows, width)


def reduce_kernel(per, rows, hid, f_ref, out_ref, tile_ref):
    pieces = f_ref.shape[0]
    groups = out_ref.shape[0]
    chunk = pieces * rows
    tile = f_ref[:, :, HALF * per :]
    tile_ref[...] = tile
    lane = iota((hid, chunk), 1) % rows
    weights, features = [], []
    for c in range(per):
        spread = jnp.broadcast_to(tile[:, c : c + 1, :], tile.shape).reshape(chunk, 128)
        spread = spread.T[:hid]
        weights.append(jnp.concatenate(
            [jnp.where(lane == k, spread, 0.0) for k in range(rows)], 0).astype(bf16))
        features.append(f_ref[:, :, HALF * c : HALF * (c + 1)].reshape(chunk, HALF))
    high, low = split(jnp.concatenate(features, 0))
    pre = mm(jnp.concatenate(weights, 1), jnp.concatenate([high, low], 1))
    pre = (pre[:, :HALF] + pre[:, HALF:]) * (1.0 / IN_SCALE)
    main = pre.shape[0] // groups
    out_ref[:, :main, :] = pre.reshape(groups, main, HALF)
    extra = jnp.zeros((pieces, 128), f32)
    for c in range(per):
        extra = extra + tile[:, c, :] * tile[:, per, c : c + 1]
    extra = jnp.sum(extra, axis=0, keepdims=True) * (1.0 / IN_SCALE)
    out_ref[:, main:, :] = jnp.broadcast_to(extra[None], (groups, 8, 128))


def gelu(v):
    return 0.5 * v * (1.0 + lax.erf(v * math.sqrt(0.5)))


def hidden_kernel(main, hid, r_ref, bias_ref, cout_ref, out_ref, gain_ref):
    groups = r_ref.shape[0]
    total = r_ref[0]
    for g in range(1, groups):
        total = total + r_ref[g]
    start = lax.axis_index("chip") * main
    bias = bias_ref[0:1]
    column = jnp.sum(
        jnp.where(iota((main, hid), 1) == (iota((main, hid), 0) + start) % hid, bias, 0.0),
        axis=1, keepdims=True)
    out_ref[...] = gelu(total[:main] + column)
    spare = gelu(total[main:, :hid] + bias)
    high, low = split(spare)
    gain_ref[...] = mm(high, cout_ref[...]) + mm(low, cout_ref[...])


def gain_kernel(per, rows, hid, h_ref, tile_ref, out_ref):
    pieces = tile_ref.shape[0]
    chunk = pieces * rows
    wide = rows * hid
    high, low = split(h_ref[...].reshape(wide, HALF))
    hidden = jnp.concatenate([high, low], 1)
    keep = iota((chunk, wide), 0) % rows == iota((chunk, wide), 1) // hid
    tile = tile_ref[...]
    for c in range(per):
        spread = jnp.broadcast_to(tile[:, c : c + 1, :], tile.shape).reshape(chunk, 128)
        spread = jnp.concatenate([spread[:, hid:]] * rows, 1)
        g = mm(jnp.where(keep, spread, 0.0).astype(bf16), hidden)
        g = (g[:, :HALF] + g[:, HALF:]) * (GAIN_SCALE / OUT_SCALE)
        out_ref[:, :, HALF * c : HALF * (c + 1)] = g.reshape(pieces, rows, HALF)


def inverse_kernel(per, block, g_ref, spec_ref, nyq_ref, gain_ref, skip_ref, r_ref,
                   inv_ref, twf_ref, last_ref, row0_ref, out_ref):
    members = r_ref.shape[0]
    width = HALF * per
    count = g_ref.shape[0] // 2
    sums = []
    for part in range(2):
        g = g_ref[part * count : (part + 1) * count].reshape(HALF, width)
        g = g * (1.0 / GAIN_SCALE)
        if part == 0:
            dc = (iota((HALF, width), 0) == 0) & (iota((HALF, width), 1) % HALF == 0)
            g = jnp.where(dc, 0.5 * g, g)
        s = spec_ref[part]
        high, low = split(jnp.concatenate([s[:HALF] * g, s[HALF:] * g], 0))
        sums.append(mm(inv_ref[0, part], high) + mm(inv_ref[0, part], low)
                    + mm(inv_ref[1, part], high))
    own = (lax.axis_index("chip") * lax.axis_size("core") + lax.axis_index("core")) * per
    lane = iota((1, 128), 1)
    cosine, sine = twf_ref[0].T, twf_ref[1].T
    shared_cos, shared_sin = row0_ref[0].T[:, 0:1], row0_ref[1].T[:, 0:1]
    lane0 = iota((RADIX, HALF), 1) == 0
    outs = []
    for c in range(per):
        cols = slice(HALF * c, HALF * (c + 1))
        top_re, top_im = sums[0][:RADIX, cols], sums[0][RADIX:, cols]
        bot_re, bot_im = sums[1][:RADIX, cols], sums[1][RADIX:, cols]
        re = jnp.where(lane0, top_re, top_re + bot_re)
        im = top_im + bot_im
        out_re = jnp.where(lane0, re, re * cosine - im * sine)
        out_im = jnp.where(lane0, bot_re * shared_cos - bot_im * shared_sin,
                           re * sine + im * cosine)
        high, low = split(jnp.concatenate([out_re, out_im], 1))
        y = nt(last_ref[0], high) + nt(last_ref[0], low) + nt(last_ref[1], high)
        mine = lane == own + c
        skip = jnp.sum(jnp.where(mine, skip_ref[0:1], 0.0), axis=1, keepdims=True)
        gain = jnp.sum(jnp.where(mine, gain_ref[0:1], 0.0), axis=1, keepdims=True)
        spare = jnp.sum(jnp.where(lane == c, nyq_ref[0:1], 0.0), axis=1, keepdims=True)
        x = r_ref[:, block * c : block * (c + 1), :].astype(f32).reshape(RADIX, RADIX)
        y = y + (spare * gain * (1.0 / SEQ)) * row0_ref[2, 0:1] + skip * x
        outs.append(y.reshape(members, block, RADIX))
    out_ref[...] = jnp.concatenate(outs, 1).astype(bf16)


def call(kernel, outs, scratch=(), flops=0, interpret=False):
    vmem = pl.BlockSpec(memory_space=pltpu.VMEM)
    many = isinstance(outs, (list, tuple))

    def run(*args):
        return pl.pallas_call(
            kernel,
            out_shape=outs,
            in_specs=[vmem] * len(args),
            out_specs=[vmem] * len(outs) if many else vmem,
            scratch_shapes=list(scratch),
            compiler_params=pltpu.CompilerParams(vmem_limit_bytes=40 * 1024 * 1024),
        )(*args)

    return run


def exchange(x, axis):
    return lax.all_to_all(x, axis, split_axis=0, concat_axis=0, tiled=True)


def on_device(signal, cond_in, cond_bias, cond_out, skip_gain):
    shape = jax.ShapeDtypeStruct
    ctx, other = ("chip", "core"), ("core", "ch")
    members = lax.axis_size(ctx)
    pieces = lax.axis_size(other)
    groups = lax.axis_size("chip")
    seq_local, chan = signal.shape
    hid = cond_in.shape[1]
    per = chan // members
    rows = RADIX // pieces
    block = seq_local // RADIX
    width = HALF * per
    t = {name: jnp.asarray(value) for name, value in tables().items()}
    halves = [pltpu.VMEM((chan * block, 128), f32)] * 2
    piece = shape((members, per * block, RADIX), bf16)

    packed = call(pack_kernel, piece, halves)(signal)
    received = exchange(packed, ctx)
    feat, spec, nyq, last, cout, bias, skip = call(
        functools.partial(forward_kernel, per, rows, block),
        [shape((pieces, rows, width + 128), f32), shape((2, RADIX, width), f32),
         shape((8, 128), f32), shape((2, RADIX, RADIX), bf16), shape((hid, chan), bf16),
         shape((8, hid), f32), shape((8, chan), f32)],
        [pltpu.VMEM((width, 2 * RADIX), bf16)] * 4)(
            received, t["first"], t["twf"], t["row0"], t["second"], t["last"],
            cond_in.T, cond_out, cond_bias.reshape(1, hid), skip_gain.reshape(1, chan))
    feat = exchange(feat.astype(f16), other).astype(f32)
    main = rows * hid // groups
    partial, tile = call(functools.partial(reduce_kernel, per, rows, hid),
                         [shape((groups, main + 8, HALF), f32),
                          shape((pieces, rows, 128), f32)])(feat)
    partial = exchange(partial.astype(f16), "chip").astype(f32)
    hidden, spare_gain = call(functools.partial(hidden_kernel, main, hid),
                              [shape((main, HALF), f32), shape((8, chan), f32)])(
                                  partial, bias, cout)
    hidden = jnp.broadcast_to(hidden.astype(f16)[None], (groups, main, HALF))
    hidden = exchange(hidden, "chip").astype(f32)
    gain = call(functools.partial(gain_kernel, per, rows, hid),
                shape((pieces, rows, width), f32))(hidden, tile)
    gain = exchange(gain.astype(f16), other).astype(f32)
    mixed = call(functools.partial(inverse_kernel, per, block), piece)(
        gain, spec, nyq, spare_gain, skip, received, t["inv"], t["twf"], last, t["row0"])
    mixed = exchange(mixed, ctx)
    return call(unpack_kernel, shape((seq_local, chan), bf16), halves)(mixed)


def solution(mesh):
    devices = mesh.devices
    cores = 2
    fine = Mesh(devices.reshape(devices.shape[0] // cores, cores, devices.shape[1]),
                ("chip", "core", "ch"))
    ctx = ("chip", "core")
    return jax.shard_map(
        on_device,
        mesh=fine,
        in_specs=(P(ctx, "ch"), P("ch", None), P(), P(None, "ch"), P("ch")),
        out_specs=P(ctx, "ch"),
        check_vma=False,
    )
```

time: 138 us -> 128 us (0.928)
  blocking collectives: 106 us -> 119 us
  waiting for transfers between devices: 12.1 us -> 0 us
  starting transfers between devices: 5.77 us -> 0 us
  local copies, waits for them, and re-layouts: 5.75 us -> 1.82 us
    all_to_all x5 -> x6, blocking collectives: 106 us -> 119 us  [exchange(): return lax.all_to_all(x, axis, split_axis=0, concat_axis=0, tiled=True)]
    all_to_all x1 -> x0, waiting for transfers between devices: 12.1 us -> none  [exchange(): return lax.all_to_all(x, axis, split_axis=0, concat_axis=0, tiled=True)]
    all_to_all x1 -> x0, starting transfers between devices: 5.77 us -> none  [exchange(): return lax.all_to_all(x, axis, split_axis=0, concat_axis=0, tiled=True)]
    unnamed x29 -> x22, local copies, waits for them, and re-layouts: 5.75 us -> 1.79 us
    pallas_call x8 -> x7, Pallas kernels: 6.75 us -> 5.95 us  [run(): pl.pallas_call(kernel, out_shape=outs, in_specs=[vmem] * len(args), out_s...]
  transfers between devices with their start and end apart: 1 -> 0, of which waited for: 1 -> 0; matrix products, arithmetic and copies ran while one was open for 0% -> 0% of each run, Pallas kernels for 1% -> 0%
where the time goes in v2:
time: 128 us; the launch traced here: 127 us
  blocking collectives  119 us (93%)
  Pallas kernels  5.95 us (5%)
  local copies, waits for them, and re-layouts  1.82 us (1%)
    all_to_all x6, blocking collectives, exchange(): return lax.all_to_all(x, axis, split_axis=0, concat_axis=0, tiled=True)  119 us
    pallas_call x7, Pallas kernels, run(): pl.pallas_call(kernel, out_shape=outs, in_specs=[vmem] * len(args), out_s...  5.95 us

profile of v2, /device:TPU:1, one launch (start us, length us, event | category | flops | bytes accessed | tf_op | source)
XLA Modules:
  0.0 127.4 jit_solution(188516355959185392)
XLA Ops:
  0.0 0.0 copy-start.2
  0.0 0.0 copy-start.3
  0.0 1.1 copy-done.3
  1.1 0.3 shard_map.109
  1.4 0.0 copy-start
  1.5 0.0 copy-start.4
  1.5 0.0 copy-start.5
  1.5 0.0 copy-start.6
  1.5 0.0 copy-start.7
  1.5 0.0 copy-start.8
  1.5 29.2 %all_to_all.30.r_ref = bf16[32,32,256]{2,1,0:T(8,128)(2,1)S(1)} all-to-all(bf16[32,32,256]{2,1,0:T(8,128)(2,1)S(1)} %shard_map.109), channel_id=1, replica_groups=mesh['chip'=16,'core'=2,'ch'=16] {'chip','core'}, dimensions={0} | all-to-all | bytes 1048576 | tf_op jit(solution)/shard_map/all_to_all | solution.py:287
  30.7 0.0 copy-start.9
  30.7 0.0 copy-start.10
  30.7 0.0 copy-done.2
  30.8 0.0 copy-done
  30.8 0.0 copy-done.4
  30.8 0.0 copy-done.5
  30.8 0.0 copy-done.6
  30.8 0.0 copy-done.7
  30.8 0.0 copy-done.8
  30.8 0.6 copy-done.9
  31.4 0.0 copy-done.10
  31.4 1.6 %shard_map.110 = (f32[32,8,640]{2,1,0:T(8,128)S(1)}, f32[2,256,512]{2,1,0:T(8,128)S(1)}, f32[8,128]{1,0:T(8,128)S(1)}, bf16[2,256,256]{2,1,0:T(8,128)(2,1)S(1)},...) custom-call(bf16[32,32,256]{2,1,0:T(8,128)(2,1)S(1)} %all_to_all.30.r_ref, ...), custom_call_target="tpu_custom_call" | custom-call | tf_op jit(solution)/shard_map/pallas_call | solution.py:274
  33.0 24.2 %all_to_all.31 = f16[32,8,640]{2,1,0:T(8,128)(2,1)S(1)} all-to-all(f16[32,8,640]{2,1,0:T(8,128)(2,1)S(1)} %convert_element_type.24), channel_id=1, replica_groups=mesh['chip'=16,'core'=2,'ch'=16] {'core','ch'}, dimensions={0} | all-to-all | bytes 655360 | tf_op jit(solution)/shard_map/all_to_all | solution.py:287
  57.3 0.5 shard_map.111
  57.8 11.6 %all_to_all.32 = f16[16,40,128]{2,1,0:T(8,128)(2,1)S(1)} all-to-all(f16[16,40,128]{2,1,0:T(8,128)(2,1)S(1)} %convert_element_type.26), channel_id=1, replica_groups=mesh['chip'=16,'core'=2,'ch'=16] {'chip'}, dimensions={0} | all-to-all | bytes 327680 | tf_op jit(solution)/shard_map/all_to_all | solution.py:287
  69.5 0.1 shard_map.112
  69.7 12.2 %all_to_all.33 = f16[16,32,128]{2,1,0:T(8,128)(2,1)S(1)} all-to-all(f16[16,32,128]{2,1,0:T(8,128)(2,1)S(1)} %broadcast_in_dim.2), channel_id=1, replica_groups=mesh['chip'=16,'core'=2,'ch'=16] {'chip'}, dimensions={0} | all-to-all | bytes 262144 | tf_op jit(solution)/shard_map/all_to_all | solution.py:287
  81.9 0.5 shard_map.113
  82.4 0.0 copy-start.1
  82.5 18.5 %all_to_all.34 = f16[32,8,512]{2,1,0:T(8,128)(2,1)S(1)} all-to-all(f16[32,8,512]{2,1,0:T(8,128)(2,1)S(1)} %convert_element_type.30), channel_id=1, replica_groups=mesh['chip'=16,'core'=2,'ch'=16] {'core','ch'}, dimensions={0} | all-to-all | bytes 524288 | tf_op jit(solution)/shard_map/all_to_all | solution.py:287
  101.0 0.1 convert_element_type.31.g_ref
  101.1 0.0 copy-done.1
  101.1 1.9 %shard_map.114 = bf16[32,32,256]{2,1,0:T(8,128)(2,1)S(1)} custom-call(f32[32,8,512]{2,1,0:T(8,128)S(1)} %convert_element_type.31.g_ref, f32[2,256,512]{2,1,0:T(8,128)S(1)} %get-tuple-element.22.spec_ref, f32[8,128]{1,0:T(8,128)S(1)} %get-tuple-element.23.nyq_ref, f32[8,128]{1,0:T(8,128)S(1)} %get-tuple-element.24.gain_ref, ...), custom_call_target="tpu_custom_call" | custom-call | tf_op jit(solution)/shard_map/pallas_call | solution.py:274
  103.0 23.4 %all_to_all.35.r_ref = bf16[32,32,256]{2,1,0:T(8,128)(2,1)S(1)} all-to-all(bf16[32,32,256]{2,1,0:T(8,128)(2,1)S(1)} %shard_map.114), channel_id=1, replica_groups=mesh['chip'=16,'core'=2,'ch'=16] {'chip','core'}, dimensions={0} | all-to-all | bytes 1048576 | tf_op jit(solution)/shard_map/all_to_all | solution.py:287
  126.3 1.1 shard_map.115
  (8 shorter events, 0.2 us)
Async XLA Ops:
  0.0 30.7 %copy-start.2 = (bf16[2,2,256,512]{3,2,1,0:T(8,128)(2,1)S(1)}, bf16[2,2,256,512]{3,2,1,0:T(8,128)(2,1)}, u32[]{:S(2)}) copy-start(bf16[2,2,256,512]{3,2,1,0:T(8,128)(2,1)} %constant.15.clone.second_ref) | copy-start | bytes 3145732
  0.0 1.1 copy-start.3
  1.4 29.3 %copy-start = (f32[3,128,256]{2,1,0:T(8,128)S(1)}, f32[3,128,256]{2,1,0:T(8,128)}, u32[]{:S(2)}) copy-start(f32[3,128,256]{2,1,0:T(8,128)} %constant.13.clone.twf_ref) | copy-start | bytes 1179652
  1.5 29.3 %copy-start.4 = (bf16[2,256,256]{2,1,0:T(8,128)(2,1)S(1)}, bf16[2,256,256]{2,1,0:T(8,128)(2,1)}, u32[]{:S(2)}) copy-start(bf16[2,256,256]{2,1,0:T(8,128)(2,1)} %constant.17.clone.last_in_ref) | copy-start | bytes 786436
  1.5 29.3 %copy-start.5 = (bf16[512,256]{1,0:T(8,128)(2,1)S(1)}, bf16[512,256]{1,0:T(8,128)(2,1)}, u32[]{:S(2)}) copy-start(bf16[512,256]{1,0:T(8,128)(2,1)} %constant.12.clone.first_ref) | copy-start | bytes 786436
  1.5 29.3 %copy-start.6 = (f32[3,8,256]{2,1,0:T(8,128)S(1)}, f32[3,8,256]{2,1,0:T(8,128)}, u32[]{:S(2)}) copy-start(f32[3,8,256]{2,1,0:T(8,128)} %constant.14.clone.row0_ref) | copy-start | bytes 73732
  1.5 29.3 %copy-start.7 = (bf16[128,64]{0,1:T(8,128)(2,1)S(1)}, bf16[128,64]{0,1:T(8,128)(2,1)}, u32[]{:S(2)}) copy-start(bf16[128,64]{0,1:T(8,128)(2,1)} %param.12) | copy-start | bytes 49156
  1.5 29.3 %copy-start.8 = (bf16[64,128]{1,0:T(8,128)(2,1)S(1)}, bf16[64,128]{1,0:T(8,128)(2,1)}, u32[]{:S(2)}) copy-start(bf16[64,128]{1,0:T(8,128)(2,1)} %cout_in_ref.1) | copy-start | bytes 49156
  30.7 0.7 copy-start.9
  30.7 0.7 copy-start.10
  82.4 18.6 %copy-start.1 = (bf16[2,2,512,256]{3,2,1,0:T(8,128)(2,1)S(1)}, bf16[2,2,512,256]{3,2,1,0:T(8,128)(2,1)}, u32[]{:S(2)}) copy-start(bf16[2,2,512,256]{3,2,1,0:T(8,128)(2,1)} %constant.16.clone.inv_ref) | copy-start | bytes 3145732

commit v3 on v2

--- a/solution.py
+++ b/solution.py
@@ -15,6 +15,8 @@
 RADIX = 256
 HALF = RADIX // 2
 SEQ = RADIX * RADIX
+STEP = 2
+TILE = 8
 GAIN_SCALE = 0.25
 IN_SCALE = 2.0**18
 OUT_SCALE = 2.0**16
@@ -48,14 +50,15 @@
     angle = tau * np.outer(n, n) / RADIX
     wre, wim = np.cos(angle), -np.sin(angle)
     full = [np.concatenate([wre, -wim], 1), np.concatenate([wim, wre], 1)]
-    second = np.stack([np.concatenate([f[:HALF] for f in full], 0),
-                       np.concatenate([f[HALF:] for f in full], 0)])
+    order = np.arange(HALF).reshape(-1, STEP).T.reshape(-1)
+    second = np.stack([np.concatenate([f[order] for f in full], 0),
+                       np.concatenate([f[HALF + order] for f in full], 0)])
     second = np.stack(split_const(second))
     vre, vim = np.cos(angle), np.sin(angle)
     inv = np.stack([
         np.concatenate([np.concatenate([vre[:, s], -vim[:, s]], 1),
                         np.concatenate([vim[:, s], vre[:, s]], 1)], 0)
-        for s in (slice(0, HALF), slice(HALF, RADIX))])
+        for s in (order, HALF + order)])
     inv = np.stack(split_const(inv))
     angle = tau * np.outer(n, k) / RADIX
     last = np.concatenate([np.cos(angle), -np.sin(angle)], 1)
@@ -79,6 +82,11 @@
 
 def iota(shape, axis):
     return lax.broadcasted_iota(jnp.int32, shape, axis)
+
+
+def first_channel(per):
+    index = lax.axis_index("xh") * lax.axis_size("y") + lax.axis_index("y")
+    return (index * lax.axis_size("core") + lax.axis_index("core")) * per
 
 
 def pack_kernel(x_ref, out_ref, left, right):
@@ -104,7 +112,7 @@
             right[pl.ds(a, chan, stride=rows), :].T.astype(bf16))
 
 
-def forward_kernel(per, rows, block, r_ref, first_ref, twf_ref, row0_ref, second_ref, last_in_ref,
+def forward_kernel(per, block, r_ref, first_ref, twf_ref, row0_ref, second_ref, last_in_ref,
                    cin_ref, cout_in_ref, bias_in_ref, skip_in_ref,
                    feat_ref, spec_ref, nyq_ref, last_ref, cout_ref, bias_ref, skip_ref,
                    hi, lo, hi2, lo2):
@@ -112,7 +120,6 @@
     cout_ref[...] = cout_in_ref[...]
     bias_ref[...] = jnp.broadcast_to(bias_in_ref[...], bias_ref.shape)
     skip_ref[...] = jnp.broadcast_to(skip_in_ref[...], skip_ref.shape)
-    pieces = feat_ref.shape[0]
     values = r_ref[...].astype(f32)
     first_row = iota((8, RADIX), 0) == 0
     spare = jnp.zeros((8, 128), f32)
@@ -142,96 +149,93 @@
         spare = jnp.where(spare_lane == c, nyq, spare)
     nyq_ref[...] = spare
     chan = cin_ref.shape[1]
-    own = (lax.axis_index("chip") * lax.axis_size("core") + lax.axis_index("core")) * per
-    row = iota((8, chan), 0)
-    select = ((iota((8, chan), 1) == own + row) & (row < per)).astype(f32).astype(bf16)
+    row = iota((TILE, chan), 0)
+    select = ((iota((TILE, chan), 1) == first_channel(per) + row) & (row < per))
+    select = select.astype(f32).astype(bf16)
     tile = jnp.concatenate([nt(select, cin_ref[...]) * IN_SCALE,
                             nt(select, cout_in_ref[...]) * OUT_SCALE], 1)
-    tile = jnp.where(iota((8, 128), 0) == per, jnp.log1p(spare * spare * (1.0 / SEQ)), tile)
-    width = HALF * per
-    feat_ref[:, :, width:] = jnp.broadcast_to(tile[None], (pieces, rows, 128))
+    tile = jnp.where(iota((TILE, 128), 0) == per, jnp.log1p(spare * spare * (1.0 / SEQ)), tile)
+    stride = 2 * TILE
+    pieces = feat_ref.shape[0] // stride
+    for r in range(TILE):
+        feat_ref[pl.ds(TILE + r, pieces, stride=stride), :] = jnp.broadcast_to(
+            tile[r : r + 1], (pieces, 128))
+    count = HALF // STEP
     for part, (h, l) in enumerate(((hi, lo), (hi2, lo2))):
         s = (nt(second_ref[0, part], h[...]) + nt(second_ref[0, part], l[...])
              + nt(second_ref[1, part], h[...]))
         spec_ref[part] = s
         re, im = s[:HALF], s[HALF:]
         feature = jnp.log1p((re * re + im * im) * (1.0 / SEQ))
-        count = HALF // rows
-        feat_ref[part * count : (part + 1) * count, :, :width] = feature.reshape(
-            count, rows, width)
-
-
-def reduce_kernel(per, rows, hid, f_ref, out_ref, tile_ref):
-    pieces = f_ref.shape[0]
-    groups = out_ref.shape[0]
-    chunk = pieces * rows
-    tile = f_ref[:, :, HALF * per :]
-    tile_ref[...] = tile
-    lane = iota((hid, chunk), 1) % rows
-    weights, features = [], []
-    for c in range(per):
-        spread = jnp.broadcast_to(tile[:, c : c + 1, :], tile.shape).reshape(chunk, 128)
-        spread = spread.T[:hid]
-        weights.append(jnp.concatenate(
-            [jnp.where(lane == k, spread, 0.0) for k in range(rows)], 0).astype(bf16))
-        features.append(f_ref[:, :, HALF * c : HALF * (c + 1)].reshape(chunk, HALF))
-    high, low = split(jnp.concatenate(features, 0))
-    pre = mm(jnp.concatenate(weights, 1), jnp.concatenate([high, low], 1))
-    pre = (pre[:, :HALF] + pre[:, HALF:]) * (1.0 / IN_SCALE)
-    main = pre.shape[0] // groups
-    out_ref[:, :main, :] = pre.reshape(groups, main, HALF)
-    extra = jnp.zeros((pieces, 128), f32)
-    for c in range(per):
-        extra = extra + tile[:, c, :] * tile[:, per, c : c + 1]
+        for c in range(per):
+            for k in range(STEP):
+                feat_ref[pl.ds(part * count * stride + STEP * c + k, count, stride=stride), :] = (
+                    feature[count * k : count * (k + 1), HALF * c : HALF * (c + 1)])
+
+
+def reduce_kernel(per, hid, f_ref, out_ref):
+    stride = 2 * TILE
+    pieces = f_ref.shape[0] // stride
+
+    def rows(r):
+        return f_ref[pl.ds(r, pieces, stride=stride), :]
+
+    weights = [rows(TILE + c) for c in range(per)]
+    left = jnp.concatenate([w.T[:hid] for w in weights], 1).astype(bf16)
+    features = jnp.concatenate(
+        [jnp.concatenate([rows(STEP * c + k) for c in range(per)], 0) for k in range(STEP)], 1)
+    high, low = split(features)
+    pre = mm(left, jnp.concatenate([high, low], 1))
+    width = STEP * HALF
+    out_ref[:hid] = (pre[:, :width] + pre[:, width:]) * (1.0 / IN_SCALE)
+    last = rows(TILE + per)
+    extra = weights[0] * last[:, 0:1]
+    for c in range(1, per):
+        extra = extra + weights[c] * last[:, c : c + 1]
     extra = jnp.sum(extra, axis=0, keepdims=True) * (1.0 / IN_SCALE)
-    out_ref[:, main:, :] = jnp.broadcast_to(extra[None], (groups, 8, 128))
+    out_ref[hid:, :128] = jnp.broadcast_to(extra, (TILE, 128))
+    out_ref[hid:, 128:] = jnp.zeros((TILE, width - 128), f32)
 
 
 def gelu(v):
     return 0.5 * v * (1.0 + lax.erf(v * math.sqrt(0.5)))
 
 
-def hidden_kernel(main, hid, r_ref, bias_ref, cout_ref, out_ref, gain_ref):
-    groups = r_ref.shape[0]
+def gain_kernel(per, hid, r_ref, f_ref, bias_ref, cout_ref, out_ref, gain_ref):
     total = r_ref[0]
-    for g in range(1, groups):
+    for g in range(1, r_ref.shape[0]):
         total = total + r_ref[g]
-    start = lax.axis_index("chip") * main
     bias = bias_ref[0:1]
-    column = jnp.sum(
-        jnp.where(iota((main, hid), 1) == (iota((main, hid), 0) + start) % hid, bias, 0.0),
-        axis=1, keepdims=True)
-    out_ref[...] = gelu(total[:main] + column)
-    spare = gelu(total[main:, :hid] + bias)
-    high, low = split(spare)
+    column = jnp.sum(jnp.where(iota((hid, hid), 1) == iota((hid, hid), 0), bias, 0.0),
+                     axis=1, keepdims=True)
+    high, low = split(gelu(total[:hid] + column))
+    hidden = jnp.concatenate([high, low], 1)
+    hidden = jnp.concatenate([jnp.zeros_like(hidden), hidden], 0)
+    stride = 2 * TILE
+    pieces = f_ref.shape[0] // stride
+    width = STEP * HALF
+    for c in range(per):
+        weights = f_ref[pl.ds(TILE + c, pieces, stride=stride), :].astype(bf16)
+        g = mm(weights, hidden)
+        g = (g[:, :width] + g[:, width:]) * (GAIN_SCALE / OUT_SCALE)
+        for k in range(STEP):
+            out_ref[pl.ds(STEP * c + k, pieces, stride=TILE), :] = g[:, HALF * k : HALF * (k + 1)]
+    high, low = split(gelu(total[hid:, :hid] + bias))
     gain_ref[...] = mm(high, cout_ref[...]) + mm(low, cout_ref[...])
-
-
-def gain_kernel(per, rows, hid, h_ref, tile_ref, out_ref):
-    pieces = tile_ref.shape[0]
-    chunk = pieces * rows
-    wide = rows * hid
-    high, low = split(h_ref[...].reshape(wide, HALF))
-    hidden = jnp.concatenate([high, low], 1)
-    keep = iota((chunk, wide), 0) % rows == iota((chunk, wide), 1) // hid
-    tile = tile_ref[...]
-    for c in range(per):
-        spread = jnp.broadcast_to(tile[:, c : c + 1, :], tile.shape).reshape(chunk, 128)
-        spread = jnp.concatenate([spread[:, hid:]] * rows, 1)
-        g = mm(jnp.where(keep, spread, 0.0).astype(bf16), hidden)
-        g = (g[:, :HALF] + g[:, HALF:]) * (GAIN_SCALE / OUT_SCALE)
-        out_ref[:, :, HALF * c : HALF * (c + 1)] = g.reshape(pieces, rows, HALF)
 
 
 def inverse_kernel(per, block, g_ref, spec_ref, nyq_ref, gain_ref, skip_ref, r_ref,
                    inv_ref, twf_ref, last_ref, row0_ref, out_ref):
     members = r_ref.shape[0]
     width = HALF * per
-    count = g_ref.shape[0] // 2
+    count = HALF // STEP
     sums = []
     for part in range(2):
-        g = g_ref[part * count : (part + 1) * count].reshape(HALF, width)
-        g = g * (1.0 / GAIN_SCALE)
+        g = jnp.concatenate([
+            jnp.concatenate([
+                g_ref[pl.ds(part * count * TILE + STEP * c + k, count, stride=TILE), :]
+                for k in range(STEP)], 0)
+            for c in range(per)], 1) * (1.0 / GAIN_SCALE)
         if part == 0:
             dc = (iota((HALF, width), 0) == 0) & (iota((HALF, width), 1) % HALF == 0)
             g = jnp.where(dc, 0.5 * g, g)
@@ -239,7 +243,7 @@
         high, low = split(jnp.concatenate([s[:HALF] * g, s[HALF:] * g], 0))
         sums.append(mm(inv_ref[0, part], high) + mm(inv_ref[0, part], low)
                     + mm(inv_ref[1, part], high))
-    own = (lax.axis_index("chip") * lax.axis_size("core") + lax.axis_index("core")) * per
+    own = first_channel(per)
     lane = iota((1, 128), 1)
     cosine, sine = twf_ref[0].T, twf_ref[1].T
     shared_cos, shared_sin = row0_ref[0].T[:, 0:1], row0_ref[1].T[:, 0:1]
@@ -289,44 +293,42 @@
 
 def on_device(signal, cond_in, cond_bias, cond_out, skip_gain):
     shape = jax.ShapeDtypeStruct
-    ctx, other = ("chip", "core"), ("core", "ch")
+    ctx, spread, line = ("xh", "y", "core"), ("y", "core", "z"), ("xh", "xl")
     members = lax.axis_size(ctx)
-    pieces = lax.axis_size(other)
-    groups = lax.axis_size("chip")
+    pieces = lax.axis_size(spread)
+    groups = lax.axis_size(line)
     seq_local, chan = signal.shape
     hid = cond_in.shape[1]
     per = chan // members
-    rows = RADIX // pieces
     block = seq_local // RADIX
     width = HALF * per
     t = {name: jnp.asarray(value) for name, value in tables().items()}
     halves = [pltpu.VMEM((chan * block, 128), f32)] * 2
     piece = shape((members, per * block, RADIX), bf16)
 
+    def send(x, axis, count):
+        x = x.astype(f16).reshape(count, -1, x.shape[-1])
+        return exchange(x, axis).astype(f32)
+
     packed = call(pack_kernel, piece, halves)(signal)
     received = exchange(packed, ctx)
     feat, spec, nyq, last, cout, bias, skip = call(
-        functools.partial(forward_kernel, per, rows, block),
-        [shape((pieces, rows, width + 128), f32), shape((2, RADIX, width), f32),
+        functools.partial(forward_kernel, per, block),
+        [shape((pieces * 2 * TILE, HALF), f32), shape((2, RADIX, width), f32),
          shape((8, 128), f32), shape((2, RADIX, RADIX), bf16), shape((hid, chan), bf16),
          shape((8, hid), f32), shape((8, chan), f32)],
         [pltpu.VMEM((width, 2 * RADIX), bf16)] * 4)(
             received, t["first"], t["twf"], t["row0"], t["second"], t["last"],
             cond_in.T, cond_out, cond_bias.reshape(1, hid), skip_gain.reshape(1, chan))
-    feat = exchange(feat.astype(f16), other).astype(f32)
-    main = rows * hid // groups
-    partial, tile = call(functools.partial(reduce_kernel, per, rows, hid),
-                         [shape((groups, main + 8, HALF), f32),
-                          shape((pieces, rows, 128), f32)])(feat)
-    partial = exchange(partial.astype(f16), "chip").astype(f32)
-    hidden, spare_gain = call(functools.partial(hidden_kernel, main, hid),
-                              [shape((main, HALF), f32), shape((8, chan), f32)])(
-                                  partial, bias, cout)
-    hidden = jnp.broadcast_to(hidden.astype(f16)[None], (groups, main, HALF))
-    hidden = exchange(hidden, "chip").astype(f32)
-    gain = call(functools.partial(gain_kernel, per, rows, hid),
-                shape((pieces, rows, width), f32))(hidden, tile)
-    gain = exchange(gain.astype(f16), other).astype(f32)
+    feat = send(feat, spread, pieces).reshape(feat.shape)
+    partial = call(functools.partial(reduce_kernel, per, hid),
+                   shape((hid + TILE, STEP * HALF), f32))(feat)
+    partial = jnp.broadcast_to(partial[None], (groups,) + partial.shape)
+    partial = send(partial, line, groups)
+    gain, spare_gain = call(functools.partial(gain_kernel, per, hid),
+                            [shape((pieces * TILE, HALF), f32), shape((8, chan), f32)])(
+                                partial, feat, bias, cout)
+    gain = send(gain, spread, pieces).reshape(gain.shape)
     mixed = call(functools.partial(inverse_kernel, per, block), piece)(
         gain, spec, nyq, spare_gain, skip, received, t["inv"], t["twf"], last, t["row0"])
     mixed = exchange(mixed, ctx)
@@ -334,15 +336,13 @@
 
 
 def solution(mesh):
-    devices = mesh.devices
-    cores = 2
-    fine = Mesh(devices.reshape(devices.shape[0] // cores, cores, devices.shape[1]),
-                ("chip", "core", "ch"))
-    ctx = ("chip", "core")
+    fine = Mesh(mesh.devices.reshape(2, -1, 2, 2, mesh.devices.shape[1] // 2),
+                ("xh", "y", "core", "xl", "z"))
+    ctx, ch = ("xh", "y", "core"), ("xl", "z")
     return jax.shard_map(
         on_device,
         mesh=fine,
-        in_specs=(P(ctx, "ch"), P("ch", None), P(), P(None, "ch"), P("ch")),
-        out_specs=P(ctx, "ch"),
+        in_specs=(P(ctx, ch), P(ch, None), P(), P(None, ch), P(ch)),
+        out_specs=P(ctx, ch),
         check_vma=False,
     )

time: 128 us -> 124 us (0.969)
  blocking collectives: 119 us -> 115 us
    all_to_all x6 -> x5, blocking collectives: 119 us -> 115 us  [exchange(): return lax.all_to_all(x, axis, split_axis=0, concat_axis=0, tiled=True)]
    pallas_call x7 -> x6, Pallas kernels: 5.95 us -> 5.95 us  [run(): pl.pallas_call(kernel, out_shape=outs, in_specs=[vmem] * len(args), out_s...]
where the time goes in v3:
time: 124 us; the launch traced here: 123 us
  blocking collectives  115 us (93%)
  Pallas kernels  5.95 us (5%)
  local copies, waits for them, and re-layouts  1.81 us (1%)
    all_to_all x5, blocking collectives, exchange(): return lax.all_to_all(x, axis, split_axis=0, concat_axis=0, tiled=True)  115 us
    pallas_call x6, Pallas kernels, run(): pl.pallas_call(kernel, out_shape=outs, in_specs=[vmem] * len(args), out_s...  5.95 us

profile of v3, /device:TPU:1, one launch (start us, length us, event | category | flops | bytes accessed | tf_op | source)
XLA Modules:
  0.0 123.4 jit_solution(11188290011771371466)
XLA Ops:
  0.0 0.0 copy-start.2
  0.0 0.0 copy-start.3
  0.0 1.1 copy-done.3
  1.1 0.3 shard_map.109
  1.4 0.0 copy-start
  1.5 0.0 copy-start.4
  1.5 0.0 copy-start.5
  1.5 0.0 copy-start.6
  1.5 0.0 copy-start.7
  1.5 0.0 copy-start.8
  1.5 29.2 %all_to_all.25.r_ref = bf16[32,32,256]{2,1,0:T(8,128)(2,1)S(1)} all-to-all(bf16[32,32,256]{2,1,0:T(8,128)(2,1)S(1)} %shard_map.109), channel_id=1, replica_groups=mesh['xh'=2,'y'=8,'core'=2,'xl'=2,'z'=8] {'xh','y','core'}, dimensions={0} | all-to-all | bytes 1048576 | tf_op jit(solution)/shard_map/all_to_all | solution.py:291
  30.7 0.0 copy-start.9
  30.7 0.0 copy-start.10
  30.7 0.0 copy-done.2
  30.8 0.0 copy-done
  30.8 0.0 copy-done.4
  30.8 0.0 copy-done.5
  30.8 0.0 copy-done.6
  30.8 0.0 copy-done.7
  30.8 0.0 copy-done.8
  30.8 0.6 copy-done.9
  31.4 0.0 copy-done.10
  31.4 1.9 %shard_map.110 = (f32[2048,128]{1,0:T(8,128)S(1)}, f32[2,256,512]{2,1,0:T(8,128)S(1)}, f32[8,128]{1,0:T(8,128)S(1)}, bf16[2,256,256]{2,1,0:T(8,128)(2,1)S(1)}, b...) custom-call(bf16[32,32,256]{2,1,0:T(8,128)(2,1)S(1)} %all_to_all.25.r_ref, ...), custom_call_target="tpu_custom_call" | custom-call | tf_op jit(solution)/shard_map/pallas_call | solution.py:278
  33.3 0.1 convert_element_type.15
  33.4 35.0 %all_to_all.26 = f16[128,16,128]{2,1,0:T(8,128)(2,1)S(1)} all-to-all(f16[128,16,128]{2,1,0:T(8,128)(2,1)S(1)} %bitcast.15), channel_id=1, replica_groups=mesh['xh'=2,'y'=8,'core'=2,'xl'=2,'z'=8] {'y','core','z'}, dimensions={0} | all-to-all | bytes 1048576 | tf_op jit(solution)/shard_map/all_to_all | solution.py:291
  68.4 0.1 bitcast_convert_fusion.f_ref
  68.6 0.4 shard_map.111
  69.0 7.7 %all_to_all.27 = f16[4,72,256]{2,1,0:T(8,128)(2,1)S(1)} all-to-all(f16[4,72,256]{2,1,0:T(8,128)(2,1)S(1)} %broadcast_in_dim.2), channel_id=1, replica_groups=mesh['xh'=2,'y'=8,'core'=2,'xl'=2,'z'=8] {'xh','xl'}, dimensions={0} | all-to-all | bytes 294912 | tf_op jit(solution)/shard_map/all_to_all | solution.py:291
  76.8 0.4 shard_map.112
  77.2 0.0 copy-start.1
  77.2 21.0 %all_to_all.28 = f16[128,8,128]{2,1,0:T(8,128)(2,1)S(1)} all-to-all(f16[128,8,128]{2,1,0:T(8,128)(2,1)S(1)} %convert_bitcast_fusion), channel_id=1, replica_groups=mesh['xh'=2,'y'=8,'core'=2,'xl'=2,'z'=8] {'y','core','z'}, dimensions={0} | all-to-all | bytes 524288 | tf_op jit(solution)/shard_map/all_to_all | solution.py:291
  98.2 0.0 copy-done.1
  98.3 1.9 %shard_map.113 = bf16[32,32,256]{2,1,0:T(8,128)(2,1)S(1)} custom-call(f32[1024,128]{1,0:T(8,128)S(1)} %bitcast_convert_fusion.1.g_ref, f32[2,256,512]{2,1,0:T(8,128)S(1)} %get-tuple-element.18.spec_ref, f32[8,128]{1,0:T(8,128)S(1)} %get-tuple-element.19.nyq_ref, f32[8,128]{1,0:T(8,128)S(1)} %get-tuple-element.20.gain_ref, ...), custom_call_target="tpu_custom_call" | custom-call | tf_op jit(solution)/shard_map/pallas_call | solution.py:278
  100.1 22.2 %all_to_all.29.r_ref = bf16[32,32,256]{2,1,0:T(8,128)(2,1)S(1)} all-to-all(bf16[32,32,256]{2,1,0:T(8,128)(2,1)S(1)} %shard_map.113), channel_id=1, replica_groups=mesh['xh'=2,'y'=8,'core'=2,'xl'=2,'z'=8] {'xh','y','core'}, dimensions={0} | all-to-all | bytes 1048576 | tf_op jit(solution)/shard_map/all_to_all | solution.py:291
  122.3 1.1 shard_map.114
  (5 shorter events, 0.1 us)
Async XLA Ops:
  0.0 30.7 %copy-start.2 = (bf16[2,2,256,512]{3,2,1,0:T(8,128)(2,1)S(1)}, bf16[2,2,256,512]{3,2,1,0:T(8,128)(2,1)}, u32[]{:S(2)}) copy-start(bf16[2,2,256,512]{3,2,1,0:T(8,128)(2,1)} %constant.15.clone.second_ref) | copy-start | bytes 3145732
  0.0 1.1 copy-start.3
  1.4 29.3 %copy-start = (f32[3,128,256]{2,1,0:T(8,128)S(1)}, f32[3,128,256]{2,1,0:T(8,128)}, u32[]{:S(2)}) copy-start(f32[3,128,256]{2,1,0:T(8,128)} %constant.13.clone.twf_ref) | copy-start | bytes 1179652
  1.5 29.3 %copy-start.4 = (bf16[2,256,256]{2,1,0:T(8,128)(2,1)S(1)}, bf16[2,256,256]{2,1,0:T(8,128)(2,1)}, u32[]{:S(2)}) copy-start(bf16[2,256,256]{2,1,0:T(8,128)(2,1)} %constant.17.clone.last_in_ref) | copy-start | bytes 786436
  1.5 29.3 %copy-start.5 = (bf16[512,256]{1,0:T(8,128)(2,1)S(1)}, bf16[512,256]{1,0:T(8,128)(2,1)}, u32[]{:S(2)}) copy-start(bf16[512,256]{1,0:T(8,128)(2,1)} %constant.12.clone.first_ref) | copy-start | bytes 786436
  1.5 29.3 %copy-start.6 = (f32[3,8,256]{2,1,0:T(8,128)S(1)}, f32[3,8,256]{2,1,0:T(8,128)}, u32[]{:S(2)}) copy-start(f32[3,8,256]{2,1,0:T(8,128)} %constant.14.clone.row0_ref) | copy-start | bytes 73732
  1.5 29.3 %copy-start.7 = (bf16[128,64]{0,1:T(8,128)(2,1)S(1)}, bf16[128,64]{0,1:T(8,128)(2,1)}, u32[]{:S(2)}) copy-start(bf16[128,64]{0,1:T(8,128)(2,1)} %param.12) | copy-start | bytes 49156
  1.5 29.3 %copy-start.8 = (bf16[64,128]{1,0:T(8,128)(2,1)S(1)}, bf16[64,128]{1,0:T(8,128)(2,1)}, u32[]{:S(2)}) copy-start(bf16[64,128]{1,0:T(8,128)(2,1)} %cout_in_ref.1) | copy-start | bytes 49156
  30.7 0.7 copy-start.9
  30.7 0.7 copy-start.10
  77.2 21.1 %copy-start.1 = (bf16[2,2,512,256]{3,2,1,0:T(8,128)(2,1)S(1)}, bf16[2,2,512,256]{3,2,1,0:T(8,128)(2,1)}, u32[]{:S(2)}) copy-start(bf16[2,2,512,256]{3,2,1,0:T(8,128)(2,1)} %constant.16.clone.inv_ref) | copy-start | bytes 3145732

commit v4 on v3

--- a/solution.py
+++ b/solution.py
@@ -29,14 +29,17 @@
 
 
 @functools.lru_cache(maxsize=None)
-def tables():
+def tables(sizes):
+    arrival = np.arange(math.prod(sizes)).reshape(sizes).transpose(1, 0, 2).reshape(-1)
+    block = RADIX // arrival.size
+    position = (arrival[:, None] * block + np.arange(block)).reshape(-1)
     n = np.arange(RADIX, dtype=np.float64)
     k = np.arange(HALF, dtype=np.float64)
     tau = 2.0 * np.pi
     angle = tau * np.outer(k, n) / RADIX
     first = np.concatenate([np.cos(angle), -np.sin(angle)], 0)
     first[HALF] = np.cos(math.pi * n)
-    first = np.concatenate(split_const(first), 0)
+    first = np.concatenate(split_const(first[:, position]), 0)
     angle = tau * np.outer(k, n) / SEQ
     cos_f, sin_f = np.cos(angle), np.sin(angle)
     cos_g = cos_f.copy()
@@ -63,7 +66,7 @@
     angle = tau * np.outer(n, k) / RADIX
     last = np.concatenate([np.cos(angle), -np.sin(angle)], 1)
     last[:, HALF] = np.cos(math.pi * n)
-    last = np.stack(split_const(last * (2.0 / SEQ)))
+    last = np.stack(split_const(last[position] * (2.0 / SEQ)))
     return dict(first=first, twf=twf, row0=row0, second=second, inv=inv, last=last)
 
 
@@ -85,41 +88,57 @@
 
 
 def first_channel(per):
-    index = lax.axis_index("xh") * lax.axis_size("y") + lax.axis_index("y")
+    index = lax.axis_index("y") * lax.axis_size("xh") + lax.axis_index("xh")
     return (index * lax.axis_size("core") + lax.axis_index("core")) * per
 
 
-def pack_kernel(x_ref, out_ref, left, right):
-    rows = x_ref.shape[0] // RADIX
+def pack_kernel(x_ref, bias_ref, skip_ref, out_ref, bias_out, skip_out, left, right, x, sems):
+    blocks = x_ref.shape[0] // RADIX
     chan = x_ref.shape[1]
-    for a in range(rows):
-        block = x_ref[RADIX * a : RADIX * (a + 1), :].astype(f32).T
-        left[pl.ds(a, chan, stride=rows), :] = block[:, :128]
-        right[pl.ds(a, chan, stride=rows), :] = block[:, 128:]
+
+    def rows(a):
+        return pl.ds(RADIX * a, RADIX)
+
+    copies = [pltpu.make_async_copy(x_ref.at[rows(a)], x.at[rows(a)], sems.at[a])
+              for a in range(blocks)]
+    copies += [pltpu.make_async_copy(bias_ref, bias_out, sems.at[blocks]),
+               pltpu.make_async_copy(skip_ref, skip_out, sems.at[blocks + 1])]
+    for copy in copies:
+        copy.start()
+    for a in range(blocks):
+        copies[a].wait()
+        block = x[RADIX * a : RADIX * (a + 1), :].astype(f32).T
+        left[pl.ds(a, chan, stride=blocks), :] = block[:, :128]
+        right[pl.ds(a, chan, stride=blocks), :] = block[:, 128:]
     out_ref[:, :, :128] = left[...].astype(bf16).reshape(out_ref.shape[:2] + (128,))
     out_ref[:, :, 128:] = right[...].astype(bf16).reshape(out_ref.shape[:2] + (128,))
-
-
-def unpack_kernel(r_ref, out_ref, left, right):
-    rows = out_ref.shape[0] // RADIX
+    for copy in copies[blocks:]:
+        copy.wait()
+
+
+def unpack_kernel(r_ref, out_ref, left, right, y, sems):
+    blocks = out_ref.shape[0] // RADIX
     chan = out_ref.shape[1]
     left[...] = r_ref[:, :, :128].astype(f32).reshape(left.shape)
     right[...] = r_ref[:, :, 128:].astype(f32).reshape(right.shape)
-    for a in range(rows):
-        out_ref[RADIX * a : RADIX * a + 128, :] = (
-            left[pl.ds(a, chan, stride=rows), :].T.astype(bf16))
-        out_ref[RADIX * a + 128 : RADIX * (a + 1), :] = (
-            right[pl.ds(a, chan, stride=rows), :].T.astype(bf16))
+    copies = []
+    for a in range(blocks):
+        y[RADIX * a : RADIX * a + 128, :] = (
+            left[pl.ds(a, chan, stride=blocks), :].T.astype(bf16))
+        y[RADIX * a + 128 : RADIX * (a + 1), :] = (
+            right[pl.ds(a, chan, stride=blocks), :].T.astype(bf16))
+        rows = pl.ds(RADIX * a, RADIX)
+        copies.append(pltpu.make_async_copy(y.at[rows], out_ref.at[rows], sems.at[a]))
+        copies[-1].start()
+    for copy in copies:
+        copy.wait()
 
 
 def forward_kernel(per, block, r_ref, first_ref, twf_ref, row0_ref, second_ref, last_in_ref,
-                   cin_ref, cout_in_ref, bias_in_ref, skip_in_ref,
-                   feat_ref, spec_ref, nyq_ref, last_ref, cout_ref, bias_ref, skip_ref,
+                   cin_ref, cout_in_ref, feat_ref, spec_ref, nyq_ref, last_ref, cout_ref,
                    hi, lo, hi2, lo2):
     last_ref[...] = last_in_ref[...]
     cout_ref[...] = cout_in_ref[...]
-    bias_ref[...] = jnp.broadcast_to(bias_in_ref[...], bias_ref.shape)
-    skip_ref[...] = jnp.broadcast_to(skip_in_ref[...], skip_ref.shape)
     values = r_ref[...].astype(f32)
     first_row = iota((8, RADIX), 0) == 0
     spare = jnp.zeros((8, 128), f32)
@@ -270,16 +289,16 @@
     out_ref[...] = jnp.concatenate(outs, 1).astype(bf16)
 
 
-def call(kernel, outs, scratch=(), flops=0, interpret=False):
-    vmem = pl.BlockSpec(memory_space=pltpu.VMEM)
+def call(kernel, outs, scratch=(), source=pltpu.VMEM, target=pltpu.VMEM):
     many = isinstance(outs, (list, tuple))
 
     def run(*args):
         return pl.pallas_call(
             kernel,
             out_shape=outs,
-            in_specs=[vmem] * len(args),
-            out_specs=[vmem] * len(outs) if many else vmem,
+            in_specs=[pl.BlockSpec(memory_space=source)] * len(args),
+            out_specs=[pl.BlockSpec(memory_space=target)] * len(outs) if many
+            else pl.BlockSpec(memory_space=target),
             scratch_shapes=list(scratch),
             compiler_params=pltpu.CompilerParams(vmem_limit_bytes=40 * 1024 * 1024),
         )(*args)
@@ -293,7 +312,7 @@
 
 def on_device(signal, cond_in, cond_bias, cond_out, skip_gain):
     shape = jax.ShapeDtypeStruct
-    ctx, spread, line = ("xh", "y", "core"), ("y", "core", "z"), ("xh", "xl")
+    ctx, spread, line = ("y", "xh", "core"), ("y", "z", "core"), ("xl", "xh")
     members = lax.axis_size(ctx)
     pieces = lax.axis_size(spread)
     groups = lax.axis_size(line)
@@ -302,24 +321,27 @@
     per = chan // members
     block = seq_local // RADIX
     width = HALF * per
-    t = {name: jnp.asarray(value) for name, value in tables().items()}
-    halves = [pltpu.VMEM((chan * block, 128), f32)] * 2
+    t = tables(tuple(lax.axis_size(name) for name in ("xh", "y", "core")))
+    t = {name: jnp.asarray(value) for name, value in t.items()}
+    buffers = [pltpu.VMEM((chan * block, 128), f32)] * 2 + [
+        pltpu.VMEM((seq_local, chan), bf16), pltpu.SemaphoreType.DMA((block + 2,))]
     piece = shape((members, per * block, RADIX), bf16)
 
     def send(x, axis, count):
         x = x.astype(f16).reshape(count, -1, x.shape[-1])
         return exchange(x, axis).astype(f32)
 
-    packed = call(pack_kernel, piece, halves)(signal)
+    packed, bias, skip = call(
+        pack_kernel, [piece, shape((1, hid), f32), shape((1, chan), f32)], buffers,
+        source=pltpu.HBM)(signal, cond_bias.reshape(1, hid), skip_gain.reshape(1, chan))
     received = exchange(packed, ctx)
-    feat, spec, nyq, last, cout, bias, skip = call(
+    feat, spec, nyq, last, cout = call(
         functools.partial(forward_kernel, per, block),
         [shape((pieces * 2 * TILE, HALF), f32), shape((2, RADIX, width), f32),
-         shape((8, 128), f32), shape((2, RADIX, RADIX), bf16), shape((hid, chan), bf16),
-         shape((8, hid), f32), shape((8, chan), f32)],
+         shape((8, 128), f32), shape((2, RADIX, RADIX), bf16), shape((hid, chan), bf16)],
         [pltpu.VMEM((width, 2 * RADIX), bf16)] * 4)(
             received, t["first"], t["twf"], t["row0"], t["second"], t["last"],
-            cond_in.T, cond_out, cond_bias.reshape(1, hid), skip_gain.reshape(1, chan))
+            cond_in.T, cond_out)
     feat = send(feat, spread, pieces).reshape(feat.shape)
     partial = call(functools.partial(reduce_kernel, per, hid),
                    shape((hid + TILE, STEP * HALF), f32))(feat)
@@ -332,7 +354,8 @@
     mixed = call(functools.partial(inverse_kernel, per, block), piece)(
         gain, spec, nyq, spare_gain, skip, received, t["inv"], t["twf"], last, t["row0"])
     mixed = exchange(mixed, ctx)
-    return call(unpack_kernel, shape((seq_local, chan), bf16), halves)(mixed)
+    return call(unpack_kernel, shape((seq_local, chan), bf16), buffers,
+                target=pltpu.HBM)(mixed)
 
 
 def solution(mesh):

time: 124 us -> 126 us (1.016)
  local copies, waits for them, and re-layouts: 1.81 us -> 4.39 us
  Pallas kernels: 5.95 us -> 7.29 us
    unnamed x22, local copies, waits for them, and re-layouts: 1.79 us -> 4.37 us
    pallas_call x6, Pallas kernels: 5.95 us -> 7.29 us  [run(): pl.pallas_call(kernel, out_shape=outs, in_specs=[pl.BlockSpec(memory_spac...]
where the time goes in v4:
time: 126 us
  blocking collectives  114 us (90%)
  Pallas kernels  7.29 us (6%)
  local copies, waits for them, and re-layouts  4.39 us (3%)
    all_to_all x5, blocking collectives, exchange(): return lax.all_to_all(x, axis, split_axis=0, concat_axis=0, tiled=True)  114 us
    pallas_call x6, Pallas kernels, run(): pl.pallas_call(kernel, out_shape=outs, in_specs=[pl.BlockSpec(memory_spac...  7.29 us
    unnamed x22, local copies, waits for them, and re-layouts  4.37 us

profile of v4, /device:TPU:1, one launch (start us, length us, event | category | flops | bytes accessed | tf_op | source)
XLA Modules:
  0.0 126.1 jit_solution(13643434950463481578)
XLA Ops:
  0.0 0.0 copy-start.2
  0.0 0.0 copy-start.3
  0.0 1.1 copy-done.3
  1.1 0.0 copy-start.9
  1.1 0.7 copy-done.9
  1.8 0.0 copy-start.10
  1.8 0.7 copy-done.10
  2.4 1.7 %shard_map.109 = (bf16[32,32,256]{2,1,0:T(8,128)(2,1)S(1)}, f32[1,64]{1,0:T(1,128)S(1)}, f32[1,128]{1,0:T(1,128)S(1)}) custom-call(bf16[2048,128]{1,0:T(8,128)(2,1)S(1)} %copy-done.3, f32[1,64]{1,0:T(1,128)S(1)} %bitcast.13, f32[1,128]{1,0:T(1,128)S(1)} %bitcast.14), custom_call_target="tpu_custom_call" | custom-call | tf_op jit(solution)/shard_map/pallas_call | solution.py:296
  4.1 0.0 copy-start
  4.1 0.0 copy-start.6
  4.2 0.0 copy-start.7
  4.2 0.0 copy-start.8
  4.2 28.2 %all_to_all.25.r_ref = bf16[32,32,256]{2,1,0:T(8,128)(2,1)S(1)} all-to-all(bf16[32,32,256]{2,1,0:T(8,128)(2,1)S(1)} %get-tuple-element.15), channel_id=1, replica_groups=mesh['xh'=2,'y'=8,'core'=2,'xl'=2,'z'=8] {'y','xh','core'}, dimensions={0} | all-to-all | bytes 1048576 | tf_op jit(solution)/shard_map/all_to_all | solution.py:310
  32.3 0.0 copy-done.2
  32.3 0.0 copy-done
  32.3 0.0 copy-done.6
  32.3 0.0 copy-done.7
  32.4 0.0 copy-done.8
  32.4 0.0 copy-start.4
  32.4 0.9 copy-done.4
  33.3 0.0 copy-start.5
  33.3 0.9 copy-done.5
  34.3 1.9 %shard_map.110 = (f32[2048,128]{1,0:T(8,128)S(1)}, f32[2,256,512]{2,1,0:T(8,128)S(1)}, f32[8,128]{1,0:T(8,128)S(1)}, bf16[2,256,256]{2,1,0:T(8,128)(2,1)S(1)}, bf16[64,128]{1,0:T(8,128)(2,1)S(1)}) custom-call(bf16[32,32,256]{2,1,0:T(8,128)(2,1)S(1)} %all_to_all.25.r_ref, bf16[512,256]{1,0:T(8,128)(2,1)S(1)} %copy-done.5, f32[3,128,256]{2,1,0:T(8,128)S(1)} %copy-done, ...), custom_call_target="tpu_custom_call" | custom-call | tf_op jit(solution)/shard_map/pallas_call | solution.py:296
  36.2 0.1 convert_element_type.15
  36.3 34.2 %all_to_all.26 = f16[128,16,128]{2,1,0:T(8,128)(2,1)S(1)} all-to-all(f16[128,16,128]{2,1,0:T(8,128)(2,1)S(1)} %bitcast.15), channel_id=1, replica_groups=mesh['xh'=2,'y'=8,'core'=2,'xl'=2,'z'=8] {'y','z','core'}, dimensions={0} | all-to-all | bytes 1048576 | tf_op jit(solution)/shard_map/all_to_all | solution.py:310
  70.4 0.1 bitcast_convert_fusion.f_ref
  70.6 0.4 shard_map.111
  71.0 7.2 %all_to_all.27 = f16[4,72,256]{2,1,0:T(8,128)(2,1)S(1)} all-to-all(f16[4,72,256]{2,1,0:T(8,128)(2,1)S(1)} %broadcast_in_dim.2), channel_id=1, replica_groups=mesh['xh'=2,'y'=8,'core'=2,'xl'=2,'z'=8] {'xl','xh'}, dimensions={0} | all-to-all | bytes 294912 | tf_op jit(solution)/shard_map/all_to_all | solution.py:310
  78.2 0.4 shard_map.112
  78.6 0.0 copy-start.1
  78.7 22.3 %all_to_all.28 = f16[128,8,128]{2,1,0:T(8,128)(2,1)S(1)} all-to-all(f16[128,8,128]{2,1,0:T(8,128)(2,1)S(1)} %convert_bitcast_fusion), channel_id=1, replica_groups=mesh['xh'=2,'y'=8,'core'=2,'xl'=2,'z'=8] {'y','z','core'}, dimensions={0} | all-to-all | bytes 524288 | tf_op jit(solution)/shard_map/all_to_all | solution.py:310
  101.0 0.0 copy-done.1
  101.0 1.9 %shard_map.113 = bf16[32,32,256]{2,1,0:T(8,128)(2,1)S(1)} custom-call(f32[1024,128]{1,0:T(8,128)S(1)} %bitcast_convert_fusion.1.g_ref, f32[2,256,512]{2,1,0:T(8,128)S(1)} %get-tuple-element.20.spec_ref, f32[8,128]{1,0:T(8,128)S(1)} %get-tuple-element.21.nyq_ref, f32[8,128]{1,0:T(8,128)S(1)} %get-tuple-element.22.gain_ref, ...), custom_call_target="tpu_custom_call" | custom-call | tf_op jit(solution)/shard_map/pallas_call | solution.py:296
  102.9 22.1 %all_to_all.29.r_ref = bf16[32,32,256]{2,1,0:T(8,128)(2,1)S(1)} all-to-all(bf16[32,32,256]{2,1,0:T(8,128)(2,1)S(1)} %shard_map.113), channel_id=1, replica_groups=mesh['xh'=2,'y'=8,'core'=2,'xl'=2,'z'=8] {'y','xh','core'}, dimensions={0} | all-to-all | bytes 1048576 | tf_op jit(solution)/shard_map/all_to_all | solution.py:310
  125.0 1.0 shard_map.114
  (5 shorter events, 0.1 us)
Async XLA Ops:
  0.0 32.3 %copy-start.2 = (bf16[2,2,256,512]{3,2,1,0:T(8,128)(2,1)S(1)}, bf16[2,2,256,512]{3,2,1,0:T(8,128)(2,1)}, u32[]{:S(2)}) copy-start(bf16[2,2,256,512]{3,2,1,0:T(8,128)(2,1)} %constant.15.clone.second_ref) | copy-start | bytes 3145732
  0.0 1.1 copy-start.3
  1.1 0.7 copy-start.9
  1.8 0.7 copy-start.10
  4.1 28.2 %copy-start = (f32[3,128,256]{2,1,0:T(8,128)S(1)}, f32[3,128,256]{2,1,0:T(8,128)}, u32[]{:S(2)}) copy-start(f32[3,128,256]{2,1,0:T(8,128)} %constant.13.clone.twf_ref) | copy-start | bytes 1179652
  4.1 28.2 %copy-start.6 = (f32[3,8,256]{2,1,0:T(8,128)S(1)}, f32[3,8,256]{2,1,0:T(8,128)}, u32[]{:S(2)}) copy-start(f32[3,8,256]{2,1,0:T(8,128)} %constant.14.clone.row0_ref) | copy-start | bytes 73732
  4.2 28.2 %copy-start.7 = (bf16[128,64]{0,1:T(8,128)(2,1)S(1)}, bf16[128,64]{0,1:T(8,128)(2,1)}, u32[]{:S(2)}) copy-start(bf16[128,64]{0,1:T(8,128)(2,1)} %param.12) | copy-start | bytes 49156
  4.2 28.2 %copy-start.8 = (bf16[64,128]{1,0:T(8,128)(2,1)S(1)}, bf16[64,128]{1,0:T(8,128)(2,1)}, u32[]{:S(2)}) copy-start(bf16[64,128]{1,0:T(8,128)(2,1)} %cout_in_ref.1) | copy-start | bytes 49156
  32.4 1.0 copy-start.4
  33.3 0.9 copy-start.5
  78.6 22.4 %copy-start.1 = (bf16[2,2,512,256]{3,2,1,0:T(8,128)(2,1)S(1)}, bf16[2,2,512,256]{3,2,1,0:T(8,128)(2,1)}, u32[]{:S(2)}) copy-start(bf16[2,2,512,256]{3,2,1,0:T(8,128)(2,1)} %constant.16.clone.inv_ref) | copy-start | bytes 3145732

commit v5 on v3

--- a/solution.py
+++ b/solution.py
@@ -29,14 +29,17 @@
 
 
 @functools.lru_cache(maxsize=None)
-def tables():
+def tables(sizes):
+    arrival = np.arange(math.prod(sizes)).reshape(sizes).transpose(1, 0, 2).reshape(-1)
+    block = RADIX // arrival.size
+    position = (arrival[:, None] * block + np.arange(block)).reshape(-1)
     n = np.arange(RADIX, dtype=np.float64)
     k = np.arange(HALF, dtype=np.float64)
     tau = 2.0 * np.pi
     angle = tau * np.outer(k, n) / RADIX
     first = np.concatenate([np.cos(angle), -np.sin(angle)], 0)
     first[HALF] = np.cos(math.pi * n)
-    first = np.concatenate(split_const(first), 0)
+    first = np.concatenate(split_const(first[:, position]), 0)
     angle = tau * np.outer(k, n) / SEQ
     cos_f, sin_f = np.cos(angle), np.sin(angle)
     cos_g = cos_f.copy()
@@ -63,7 +66,7 @@
     angle = tau * np.outer(n, k) / RADIX
     last = np.concatenate([np.cos(angle), -np.sin(angle)], 1)
     last[:, HALF] = np.cos(math.pi * n)
-    last = np.stack(split_const(last * (2.0 / SEQ)))
+    last = np.stack(split_const(last[position] * (2.0 / SEQ)))
     return dict(first=first, twf=twf, row0=row0, second=second, inv=inv, last=last)
 
 
@@ -85,7 +88,7 @@
 
 
 def first_channel(per):
-    index = lax.axis_index("xh") * lax.axis_size("y") + lax.axis_index("y")
+    index = lax.axis_index("y") * lax.axis_size("xh") + lax.axis_index("xh")
     return (index * lax.axis_size("core") + lax.axis_index("core")) * per
 
 
@@ -293,7 +296,7 @@
 
 def on_device(signal, cond_in, cond_bias, cond_out, skip_gain):
     shape = jax.ShapeDtypeStruct
-    ctx, spread, line = ("xh", "y", "core"), ("y", "core", "z"), ("xh", "xl")
+    ctx, spread, line = ("y", "xh", "core"), ("y", "z", "core"), ("xl", "xh")
     members = lax.axis_size(ctx)
     pieces = lax.axis_size(spread)
     groups = lax.axis_size(line)
@@ -302,7 +305,8 @@
     per = chan // members
     block = seq_local // RADIX
     width = HALF * per
-    t = {name: jnp.asarray(value) for name, value in tables().items()}
+    t = tables(tuple(lax.axis_size(name) for name in ("xh", "y", "core")))
+    t = {name: jnp.asarray(value) for name, value in t.items()}
     halves = [pltpu.VMEM((chan * block, 128), f32)] * 2
     piece = shape((members, per * block, RADIX), bf16)
 

time: 124 us -> 122 us (0.984)
  no operation moved by 1% of the time
where the time goes in v5:
time: 122 us
  blocking collectives  114 us (93%)
  Pallas kernels  5.95 us (5%)
  local copies, waits for them, and re-layouts  1.81 us (1%)
    all_to_all x5, blocking collectives, exchange(): return lax.all_to_all(x, axis, split_axis=0, concat_axis=0, tiled=True)  114 us
    pallas_call x6, Pallas kernels, run(): pl.pallas_call(kernel, out_shape=outs, in_specs=[vmem] * len(args), out_s...  5.95 us

profile of v5, /device:TPU:1, one launch (start us, length us, event | category | flops | bytes accessed | tf_op | source)
XLA Modules:
  0.0 122.2 jit_solution(7559829966872739563)
XLA Ops:
  0.0 0.0 copy-start.2
  0.0 0.0 copy-start.3
  0.0 1.1 copy-done.3
  1.1 0.3 shard_map.109
  1.4 0.0 copy-start
  1.5 0.0 copy-start.4
  1.5 0.0 copy-start.5
  1.5 0.0 copy-start.6
  1.5 0.0 copy-start.7
  1.5 0.0 copy-start.8
  1.5 28.2 %all_to_all.25.r_ref = bf16[32,32,256]{2,1,0:T(8,128)(2,1)S(1)} all-to-all(bf16[32,32,256]{2,1,0:T(8,128)(2,1)S(1)} %shard_map.109), channel_id=1, replica_groups=mesh['xh'=2,'y'=8,'core'=2,'xl'=2,'z'=8] {'y','xh','core'}, dimensions={0} | all-to-all | bytes 1048576 | tf_op jit(solution)/shard_map/all_to_all | solution.py:294
  29.7 0.0 copy-start.9
  29.7 0.0 copy-start.10
  29.7 0.0 copy-done.2
  29.7 0.0 copy-done
  29.7 0.0 copy-done.4
  29.7 0.0 copy-done.5
  29.7 0.0 copy-done.6
  29.7 0.0 copy-done.7
  29.7 0.0 copy-done.8
  29.7 0.6 copy-done.9
  30.3 0.0 copy-done.10
  30.4 1.9 %shard_map.110 = (f32[2048,128]{1,0:T(8,128)S(1)}, f32[2,256,512]{2,1,0:T(8,128)S(1)}, f32[8,128]{1,0:T(8,128)S(1)}, bf16[2,256,256]{2,1,0:T(8,128)(2,1)S(1)}, b...) custom-call(bf16[32,32,256]{2,1,0:T(8,128)(2,1)S(1)} %all_to_all.25.r_ref, ...), custom_call_target="tpu_custom_call" | custom-call | tf_op jit(solution)/shard_map/pallas_call | solution.py:281
  32.3 0.1 convert_element_type.15
  32.4 34.2 %all_to_all.26 = f16[128,16,128]{2,1,0:T(8,128)(2,1)S(1)} all-to-all(f16[128,16,128]{2,1,0:T(8,128)(2,1)S(1)} %bitcast.15), channel_id=1, replica_groups=mesh['xh'=2,'y'=8,'core'=2,'xl'=2,'z'=8] {'y','z','core'}, dimensions={0} | all-to-all | bytes 1048576 | tf_op jit(solution)/shard_map/all_to_all | solution.py:294
  66.5 0.1 bitcast_convert_fusion.f_ref
  66.6 0.4 shard_map.111
  67.1 7.2 %all_to_all.27 = f16[4,72,256]{2,1,0:T(8,128)(2,1)S(1)} all-to-all(f16[4,72,256]{2,1,0:T(8,128)(2,1)S(1)} %broadcast_in_dim.2), channel_id=1, replica_groups=mesh['xh'=2,'y'=8,'core'=2,'xl'=2,'z'=8] {'xl','xh'}, dimensions={0} | all-to-all | bytes 294912 | tf_op jit(solution)/shard_map/all_to_all | solution.py:294
  74.3 0.4 shard_map.112
  74.7 0.0 copy-start.1
  74.8 22.3 %all_to_all.28 = f16[128,8,128]{2,1,0:T(8,128)(2,1)S(1)} all-to-all(f16[128,8,128]{2,1,0:T(8,128)(2,1)S(1)} %convert_bitcast_fusion), channel_id=1, replica_groups=mesh['xh'=2,'y'=8,'core'=2,'xl'=2,'z'=8] {'y','z','core'}, dimensions={0} | all-to-all | bytes 524288 | tf_op jit(solution)/shard_map/all_to_all | solution.py:294
  97.1 0.0 copy-done.1
  97.1 1.9 %shard_map.113 = bf16[32,32,256]{2,1,0:T(8,128)(2,1)S(1)} custom-call(f32[1024,128]{1,0:T(8,128)S(1)} %bitcast_convert_fusion.1.g_ref, f32[2,256,512]{2,1,0:T(8,128)S(1)} %get-tuple-element.18.spec_ref, f32[8,128]{1,0:T(8,128)S(1)} %get-tuple-element.19.nyq_ref, f32[8,128]{1,0:T(8,128)S(1)} %get-tuple-element.20.gain_ref, ...), custom_call_target="tpu_custom_call" | custom-call | tf_op jit(solution)/shard_map/pallas_call | solution.py:281
  98.9 22.1 %all_to_all.29.r_ref = bf16[32,32,256]{2,1,0:T(8,128)(2,1)S(1)} all-to-all(bf16[32,32,256]{2,1,0:T(8,128)(2,1)S(1)} %shard_map.113), channel_id=1, replica_groups=mesh['xh'=2,'y'=8,'core'=2,'xl'=2,'z'=8] {'y','xh','core'}, dimensions={0} | all-to-all | bytes 1048576 | tf_op jit(solution)/shard_map/all_to_all | solution.py:294
  121.1 1.1 shard_map.114
  (5 shorter events, 0.1 us)
Async XLA Ops:
  0.0 29.7 %copy-start.2 = (bf16[2,2,256,512]{3,2,1,0:T(8,128)(2,1)S(1)}, bf16[2,2,256,512]{3,2,1,0:T(8,128)(2,1)}, u32[]{:S(2)}) copy-start(bf16[2,2,256,512]{3,2,1,0:T(8,128)(2,1)} %constant.15.clone.second_ref) | copy-start | bytes 3145732
  0.0 1.1 copy-start.3
  1.4 28.2 %copy-start = (f32[3,128,256]{2,1,0:T(8,128)S(1)}, f32[3,128,256]{2,1,0:T(8,128)}, u32[]{:S(2)}) copy-start(f32[3,128,256]{2,1,0:T(8,128)} %constant.13.clone.twf_ref) | copy-start | bytes 1179652
  1.5 28.2 %copy-start.4 = (bf16[2,256,256]{2,1,0:T(8,128)(2,1)S(1)}, bf16[2,256,256]{2,1,0:T(8,128)(2,1)}, u32[]{:S(2)}) copy-start(bf16[2,256,256]{2,1,0:T(8,128)(2,1)} %constant.17.clone.last_in_ref) | copy-start | bytes 786436
  1.5 28.2 %copy-start.5 = (bf16[512,256]{1,0:T(8,128)(2,1)S(1)}, bf16[512,256]{1,0:T(8,128)(2,1)}, u32[]{:S(2)}) copy-start(bf16[512,256]{1,0:T(8,128)(2,1)} %constant.12.clone.first_ref) | copy-start | bytes 786436
  1.5 28.2 %copy-start.6 = (f32[3,8,256]{2,1,0:T(8,128)S(1)}, f32[3,8,256]{2,1,0:T(8,128)}, u32[]{:S(2)}) copy-start(f32[3,8,256]{2,1,0:T(8,128)} %constant.14.clone.row0_ref) | copy-start | bytes 73732
  1.5 28.2 %copy-start.7 = (bf16[128,64]{0,1:T(8,128)(2,1)S(1)}, bf16[128,64]{0,1:T(8,128)(2,1)}, u32[]{:S(2)}) copy-start(bf16[128,64]{0,1:T(8,128)(2,1)} %param.12) | copy-start | bytes 49156
  1.5 28.2 %copy-start.8 = (bf16[64,128]{1,0:T(8,128)(2,1)S(1)}, bf16[64,128]{1,0:T(8,128)(2,1)}, u32[]{:S(2)}) copy-start(bf16[64,128]{1,0:T(8,128)(2,1)} %cout_in_ref.1) | copy-start | bytes 49156
  29.7 0.7 copy-start.9
  29.7 0.7 copy-start.10
  74.7 22.4 %copy-start.1 = (bf16[2,2,512,256]{3,2,1,0:T(8,128)(2,1)S(1)}, bf16[2,2,512,256]{3,2,1,0:T(8,128)(2,1)}, u32[]{:S(2)}) copy-start(bf16[2,2,512,256]{3,2,1,0:T(8,128)(2,1)} %constant.16.clone.inv_ref) | copy-start | bytes 3145732

commit v6 on v5

--- a/solution.py
+++ b/solution.py
@@ -16,7 +16,7 @@
 HALF = RADIX // 2
 SEQ = RADIX * RADIX
 STEP = 2
-TILE = 8
+TILE, REST = 8, 6
 GAIN_SCALE = 0.25
 IN_SCALE = 2.0**18
 OUT_SCALE = 2.0**16
@@ -49,7 +49,7 @@
     row0 = np.zeros((3, 8, RADIX))
     row0[0, 0], row0[1, 0] = np.cos(shared), np.sin(shared)
     row0[2, :] = np.cos(math.pi * n)
-    row0 = row0.astype(np.float32)
+    twf = np.concatenate([twf, row0.astype(np.float32)], 1)
     angle = tau * np.outer(n, n) / RADIX
     wre, wim = np.cos(angle), -np.sin(angle)
     full = [np.concatenate([wre, -wim], 1), np.concatenate([wim, wre], 1)]
@@ -66,8 +66,9 @@
     angle = tau * np.outer(n, k) / RADIX
     last = np.concatenate([np.cos(angle), -np.sin(angle)], 1)
     last[:, HALF] = np.cos(math.pi * n)
-    last = np.stack(split_const(last[position] * (2.0 / SEQ)))
-    return dict(first=first, twf=twf, row0=row0, second=second, inv=inv, last=last)
+    last = np.concatenate(split_const(last[position] * (2.0 / SEQ)), 0)
+    ends = np.stack([first, last])
+    return dict(ends=ends, twf=twf, second=second, inv=inv)
 
 
 def split(x):
@@ -115,11 +116,10 @@
             right[pl.ds(a, chan, stride=rows), :].T.astype(bf16))
 
 
-def forward_kernel(per, block, r_ref, first_ref, twf_ref, row0_ref, second_ref, last_in_ref,
+def forward_kernel(per, block, r_ref, ends_ref, twf_ref, second_ref,
                    cin_ref, cout_in_ref, bias_in_ref, skip_in_ref,
-                   feat_ref, spec_ref, nyq_ref, last_ref, cout_ref, bias_ref, skip_ref,
+                   feat_ref, spec_ref, nyq_ref, cout_ref, bias_ref, skip_ref,
                    hi, lo, hi2, lo2):
-    last_ref[...] = last_in_ref[...]
     cout_ref[...] = cout_in_ref[...]
     bias_ref[...] = jnp.broadcast_to(bias_in_ref[...], bias_ref.shape)
     skip_ref[...] = jnp.broadcast_to(skip_in_ref[...], skip_ref.shape)
@@ -129,11 +129,11 @@
     spare_lane = iota((8, 128), 1)
     for c in range(per):
         x = values[:, block * c : block * (c + 1), :].reshape(RADIX, RADIX).astype(bf16)
-        a = mm(first_ref[...], x)
+        a = mm(ends_ref[0], x)
         a = a[:RADIX] + a[RADIX:]
         re, im = a[:HALF], a[HALF:]
-        out_re = re * twf_ref[0] + im * twf_ref[1]
-        out_im = im * twf_ref[2] - re * twf_ref[1]
+        out_re = re * twf_ref[0, :HALF] + im * twf_ref[1, :HALF]
+        out_im = im * twf_ref[2, :HALF] - re * twf_ref[1, :HALF]
         place = pl.ds(HALF * c, HALF)
         for at, part in ((0, out_re), (RADIX, out_im)):
             high, low = split(part)
@@ -142,13 +142,13 @@
         lead = im[0:8]
         top = pl.ds(HALF * c, 16)
         alt_re = jnp.concatenate(
-            [jnp.where(first_row, lead * row0_ref[0], out_re[0:8]), out_re[8:16]], 0)
+            [jnp.where(first_row, lead * twf_ref[0, HALF:], out_re[0:8]), out_re[8:16]], 0)
         alt_im = jnp.concatenate(
-            [jnp.where(first_row, -lead * row0_ref[1], out_im[0:8]), out_im[8:16]], 0)
+            [jnp.where(first_row, -lead * twf_ref[1, HALF:], out_im[0:8]), out_im[8:16]], 0)
         for at, part in ((0, alt_re), (RADIX, alt_im)):
             high, low = split(part)
             hi2[top, at : at + RADIX], lo2[top, at : at + RADIX] = high, low
-        nyq = jnp.sum(re[0:1] * row0_ref[2, 0:1], axis=1, keepdims=True)
+        nyq = jnp.sum(re[0:1] * twf_ref[2, HALF : HALF + 1], axis=1, keepdims=True)
         spare = jnp.where(spare_lane == c, nyq, spare)
     nyq_ref[...] = spare
     chan = cin_ref.shape[1]
@@ -158,9 +158,9 @@
     tile = jnp.concatenate([nt(select, cin_ref[...]) * IN_SCALE,
                             nt(select, cout_in_ref[...]) * OUT_SCALE], 1)
     tile = jnp.where(iota((TILE, 128), 0) == per, jnp.log1p(spare * spare * (1.0 / SEQ)), tile)
-    stride = 2 * TILE
+    stride = TILE + REST
     pieces = feat_ref.shape[0] // stride
-    for r in range(TILE):
+    for r in range(REST):
         feat_ref[pl.ds(TILE + r, pieces, stride=stride), :] = jnp.broadcast_to(
             tile[r : r + 1], (pieces, 128))
     count = HALF // STEP
@@ -177,7 +177,7 @@
 
 
 def reduce_kernel(per, hid, f_ref, out_ref):
-    stride = 2 * TILE
+    stride = TILE + REST
     pieces = f_ref.shape[0] // stride
 
     def rows(r):
@@ -214,7 +214,7 @@
     high, low = split(gelu(total[:hid] + column))
     hidden = jnp.concatenate([high, low], 1)
     hidden = jnp.concatenate([jnp.zeros_like(hidden), hidden], 0)
-    stride = 2 * TILE
+    stride = TILE + REST
     pieces = f_ref.shape[0] // stride
     width = STEP * HALF
     for c in range(per):
@@ -228,7 +228,7 @@
 
 
 def inverse_kernel(per, block, g_ref, spec_ref, nyq_ref, gain_ref, skip_ref, r_ref,
-                   inv_ref, twf_ref, last_ref, row0_ref, out_ref):
+                   inv_ref, twf_ref, ends_ref, out_ref):
     members = r_ref.shape[0]
     width = HALF * per
     count = HALF // STEP
@@ -248,8 +248,8 @@
                     + mm(inv_ref[1, part], high))
     own = first_channel(per)
     lane = iota((1, 128), 1)
-    cosine, sine = twf_ref[0].T, twf_ref[1].T
-    shared_cos, shared_sin = row0_ref[0].T[:, 0:1], row0_ref[1].T[:, 0:1]
+    cosine, sine = twf_ref[0, :HALF].T, twf_ref[1, :HALF].T
+    shared_cos, shared_sin = twf_ref[0, HALF:].T[:, 0:1], twf_ref[1, HALF:].T[:, 0:1]
     lane0 = iota((RADIX, HALF), 1) == 0
     outs = []
     for c in range(per):
@@ -262,13 +262,14 @@
         out_im = jnp.where(lane0, bot_re * shared_cos - bot_im * shared_sin,
                            re * sine + im * cosine)
         high, low = split(jnp.concatenate([out_re, out_im], 1))
-        y = nt(last_ref[0], high) + nt(last_ref[0], low) + nt(last_ref[1], high)
+        y = (nt(ends_ref[1, :RADIX], high) + nt(ends_ref[1, :RADIX], low)
+             + nt(ends_ref[1, RADIX:], high))
         mine = lane == own + c
         skip = jnp.sum(jnp.where(mine, skip_ref[0:1], 0.0), axis=1, keepdims=True)
         gain = jnp.sum(jnp.where(mine, gain_ref[0:1], 0.0), axis=1, keepdims=True)
         spare = jnp.sum(jnp.where(lane == c, nyq_ref[0:1], 0.0), axis=1, keepdims=True)
         x = r_ref[:, block * c : block * (c + 1), :].astype(f32).reshape(RADIX, RADIX)
-        y = y + (spare * gain * (1.0 / SEQ)) * row0_ref[2, 0:1] + skip * x
+        y = y + (spare * gain * (1.0 / SEQ)) * twf_ref[2, HALF : HALF + 1] + skip * x
         outs.append(y.reshape(members, block, RADIX))
     out_ref[...] = jnp.concatenate(outs, 1).astype(bf16)
 
@@ -310,31 +311,30 @@
     halves = [pltpu.VMEM((chan * block, 128), f32)] * 2
     piece = shape((members, per * block, RADIX), bf16)
 
-    def send(x, axis, count):
-        x = x.astype(f16).reshape(count, -1, x.shape[-1])
-        return exchange(x, axis).astype(f32)
+    def send(x, axis, dims):
+        return exchange(x.astype(f16).reshape(dims), axis).astype(f32).reshape(x.shape)
 
     packed = call(pack_kernel, piece, halves)(signal)
     received = exchange(packed, ctx)
-    feat, spec, nyq, last, cout, bias, skip = call(
+    feat, spec, nyq, cout, bias, skip = call(
         functools.partial(forward_kernel, per, block),
-        [shape((pieces * 2 * TILE, HALF), f32), shape((2, RADIX, width), f32),
-         shape((8, 128), f32), shape((2, RADIX, RADIX), bf16), shape((hid, chan), bf16),
+        [shape((pieces * (TILE + REST), HALF), f32), shape((2, RADIX, width), f32),
+         shape((8, 128), f32), shape((hid, chan), bf16),
          shape((8, hid), f32), shape((8, chan), f32)],
         [pltpu.VMEM((width, 2 * RADIX), bf16)] * 4)(
-            received, t["first"], t["twf"], t["row0"], t["second"], t["last"],
+            received, t["ends"], t["twf"], t["second"],
             cond_in.T, cond_out, cond_bias.reshape(1, hid), skip_gain.reshape(1, chan))
-    feat = send(feat, spread, pieces).reshape(feat.shape)
+    feat = send(feat, spread, (pieces, (TILE + REST) // 2, 2, HALF))
     partial = call(functools.partial(reduce_kernel, per, hid),
                    shape((hid + TILE, STEP * HALF), f32))(feat)
     partial = jnp.broadcast_to(partial[None], (groups,) + partial.shape)
-    partial = send(partial, line, groups)
+    partial = send(partial, line, partial.shape)
     gain, spare_gain = call(functools.partial(gain_kernel, per, hid),
                             [shape((pieces * TILE, HALF), f32), shape((8, chan), f32)])(
                                 partial, feat, bias, cout)
-    gain = send(gain, spread, pieces).reshape(gain.shape)
+    gain = send(gain, spread, (pieces, TILE, HALF))
     mixed = call(functools.partial(inverse_kernel, per, block), piece)(
-        gain, spec, nyq, spare_gain, skip, received, t["inv"], t["twf"], last, t["row0"])
+        gain, spec, nyq, spare_gain, skip, received, t["inv"], t["twf"], t["ends"])
     mixed = exchange(mixed, ctx)
     return call(unpack_kernel, shape((seq_local, chan), bf16), halves)(mixed)
 

time: 122 us -> 121 us (level)
    all_to_all x5, blocking collectives: 114 us -> 113 us  [exchange(): return lax.all_to_all(x, axis, split_axis=0, concat_axis=0, tiled=True)]
where the time goes in v6:
time: 121 us; the launch traced here: 120 us
  blocking collectives  113 us (93%)
  Pallas kernels  5.44 us (4%)
  local copies, waits for them, and re-layouts  1.81 us (1%)
    all_to_all x5, blocking collectives, exchange(): return lax.all_to_all(x, axis, split_axis=0, concat_axis=0, tiled=True)  113 us
    pallas_call x6, Pallas kernels, run(): pl.pallas_call(kernel, out_shape=outs, in_specs=[vmem] * len(args), out_s...  5.44 us

profile of v6, /device:TPU:1, one launch (start us, length us, event | category | flops | bytes accessed | tf_op | source)
XLA Modules:
  0.0 120.2 jit_solution(5177199160293535462)
XLA Ops:
  0.0 0.0 copy-start.2
  0.0 0.0 copy-start.4
  0.0 1.1 copy-done.4
  1.1 0.3 shard_map.91
  1.4 0.0 copy-start
  1.5 0.0 copy-start.1
  1.5 0.0 copy-start.5
  1.5 0.0 copy-start.6
  1.5 28.2 %all_to_all.25.r_ref = bf16[32,32,256]{2,1,0:T(8,128)(2,1)S(1)} all-to-all(bf16[32,32,256]{2,1,0:T(8,128)(2,1)S(1)} %shard_map.91), channel_id=1, replica_groups=mesh['xh'=2,'y'=8,'core'=2,'xl'=2,'z'=8] {'y','xh','core'}, dimensions={0} | all-to-all | bytes 1048576 | tf_op jit(solution)/shard_map/all_to_all | solution.py:295
  29.7 0.0 copy-start.7
  29.7 0.0 copy-start.8
  29.7 0.0 copy-done.2
  29.7 0.0 copy-done
  29.7 0.0 copy-done.1
  29.7 0.0 copy-done.5
  29.7 0.0 copy-done.6
  29.7 0.6 copy-done.7
  30.3 0.0 copy-done.8
  30.3 1.6 %shard_map.92 = (f32[1792,128]{1,0:T(8,128)S(1)}, f32[2,256,512]{2,1,0:T(8,128)S(1)}, f32[8,128]{1,0:T(8,128)S(1)}, bf16[64,128]{1,0:T(8,128)(2,1)S(1)}, f32[8,64]{1,0:T(8,128)S(1)}, /*index=5*/f32[8,128]{1,0:T(8,128)S(1)}) custom-call(bf16[32,32,256]{2,1,0:T(8,128)(2,1)S(1)} %all_to_all.25.r_ref, bf16[2,512,256]{2,1,0:T(8,128)(2,1)S(1)} %copy-done, ...), custom_call_target="tpu_custom_call" | custom-call | tf_op jit(solution)/shard_map/pallas_call | solution.py:282
  31.9 0.1 convert_element_type.15
  32.0 33.0 %all_to_all.26 = f16[128,7,2,128]{3,2,1,0:T(2,128)(2,1)S(1)} all-to-all(f16[128,7,2,128]{3,2,1,0:T(2,128)(2,1)S(1)} %bitcast.14), channel_id=1, replica_groups=mesh['xh'=2,'y'=8,'core'=2,'xl'=2,'z'=8] {'y','z','core'}, dimensions={0} | all-to-all | bytes 917504 | tf_op jit(solution)/shard_map/all_to_all | solution.py:295
  64.9 0.1 convert.2.f_ref
  65.0 0.2 shard_map.93
  65.3 7.2 %all_to_all.27 = f16[4,72,256]{2,1,0:T(8,128)(2,1)S(1)} all-to-all(f16[4,72,256]{2,1,0:T(8,128)(2,1)S(1)} %broadcast_in_dim.2), channel_id=1, replica_groups=mesh['xh'=2,'y'=8,'core'=2,'xl'=2,'z'=8] {'xl','xh'}, dimensions={0} | all-to-all | bytes 294912 | tf_op jit(solution)/shard_map/all_to_all | solution.py:295
  72.5 0.4 shard_map.94
  72.9 0.0 copy-start.3
  73.0 22.1 %all_to_all.28 = f16[128,8,128]{2,1,0:T(8,128)(2,1)S(1)} all-to-all(f16[128,8,128]{2,1,0:T(8,128)(2,1)S(1)} %convert_bitcast_fusion), channel_id=1, replica_groups=mesh['xh'=2,'y'=8,'core'=2,'xl'=2,'z'=8] {'y','z','core'}, dimensions={0} | all-to-all | bytes 524288 | tf_op jit(solution)/shard_map/all_to_all | solution.py:295
  95.1 0.0 copy-done.3
  95.1 1.9 %shard_map.95 = bf16[32,32,256]{2,1,0:T(8,128)(2,1)S(1)} custom-call(f32[1024,128]{1,0:T(8,128)S(1)} %bitcast_convert_fusion.g_ref, f32[2,256,512]{2,1,0:T(8,128)S(1)} %get-tuple-element.17.spec_ref, f32[8,128]{1,0:T(8,128)S(1)} %get-tuple-element.18.nyq_ref, f32[8,128]{1,0:T(8,128)S(1)} %get-tuple-element.19.gain_ref, ...), custom_call_target="tpu_custom_call" | custom-call | tf_op jit(solution)/shard_map/pallas_call | solution.py:282
  97.0 22.1 %all_to_all.29.r_ref = bf16[32,32,256]{2,1,0:T(8,128)(2,1)S(1)} all-to-all(bf16[32,32,256]{2,1,0:T(8,128)(2,1)S(1)} %shard_map.95), channel_id=1, replica_groups=mesh['xh'=2,'y'=8,'core'=2,'xl'=2,'z'=8] {'y','xh','core'}, dimensions={0} | all-to-all | bytes 1048576 | tf_op jit(solution)/shard_map/all_to_all | solution.py:295
  119.1 1.1 shard_map.96
  (5 shorter events, 0.1 us)
Async XLA Ops:
  0.0 29.7 %copy-start.2 = (bf16[2,2,256,512]{3,2,1,0:T(8,128)(2,1)S(1)}, bf16[2,2,256,512]{3,2,1,0:T(8,128)(2,1)}, u32[]{:S(2)}) copy-start(bf16[2,2,256,512]{3,2,1,0:T(8,128)(2,1)} %constant.10.clone.second_ref) | copy-start | bytes 3145732
  0.0 1.1 copy-start.4
  1.4 28.2 %copy-start = (bf16[2,512,256]{2,1,0:T(8,128)(2,1)S(1)}, bf16[2,512,256]{2,1,0:T(8,128)(2,1)}, u32[]{:S(2)}) copy-start(bf16[2,512,256]{2,1,0:T(8,128)(2,1)} %constant.8.clone.ends_ref) | copy-start | bytes 1572868
  1.5 28.2 %copy-start.1 = (f32[3,136,256]{2,1,0:T(8,128)S(1)}, f32[3,136,256]{2,1,0:T(8,128)}, u32[]{:S(2)}) copy-start(f32[3,136,256]{2,1,0:T(8,128)} %constant.9.clone.twf_ref) | copy-start | bytes 1253380
  1.5 28.2 %copy-start.5 = (bf16[128,64]{0,1:T(8,128)(2,1)S(1)}, bf16[128,64]{0,1:T(8,128)(2,1)}, u32[]{:S(2)}) copy-start(bf16[128,64]{0,1:T(8,128)(2,1)} %param.10) | copy-start | bytes 49156
  1.5 28.2 %copy-start.6 = (bf16[64,128]{1,0:T(8,128)(2,1)S(1)}, bf16[64,128]{1,0:T(8,128)(2,1)}, u32[]{:S(2)}) copy-start(bf16[64,128]{1,0:T(8,128)(2,1)} %cout_in_ref.1) | copy-start | bytes 49156
  29.7 0.7 copy-start.7
  29.7 0.7 copy-start.8
  72.9 22.2 %copy-start.3 = (bf16[2,2,512,256]{3,2,1,0:T(8,128)(2,1)S(1)}, bf16[2,2,512,256]{3,2,1,0:T(8,128)(2,1)}, u32[]{:S(2)}) copy-start(bf16[2,2,512,256]{3,2,1,0:T(8,128)(2,1)} %constant.11.clone.inv_ref) | copy-start | bytes 3145732

commit v7 on v6

--- a/solution.py
+++ b/solution.py
@@ -297,7 +297,7 @@
 
 def on_device(signal, cond_in, cond_bias, cond_out, skip_gain):
     shape = jax.ShapeDtypeStruct
-    ctx, spread, line = ("y", "xh", "core"), ("y", "z", "core"), ("xl", "xh")
+    ctx, spread, line = ("y", "xh", "core"), ("z", "core", "y"), ("xl", "xh")
     members = lax.axis_size(ctx)
     pieces = lax.axis_size(spread)
     groups = lax.axis_size(line)

time: 121 us -> 120 us (level)
  no operation moved by 1% of the time
where the time goes in v7:
time: 120 us
  blocking collectives  112 us (93%)
  Pallas kernels  5.44 us (5%)
  local copies, waits for them, and re-layouts  1.81 us (2%)
    all_to_all x5, blocking collectives, exchange(): return lax.all_to_all(x, axis, split_axis=0, concat_axis=0, tiled=True)  112 us
    pallas_call x6, Pallas kernels, run(): pl.pallas_call(kernel, out_shape=outs, in_specs=[vmem] * len(args), out_s...  5.44 us

profile of v7, /device:TPU:1, one launch (start us, length us, event | category | flops | bytes accessed | tf_op | source)
XLA Modules:
  0.0 120.0 jit_solution(6397623169842558426)
XLA Ops:
  0.0 0.0 copy-start.2
  0.0 0.0 copy-start.4
  0.0 1.1 copy-done.4
  1.1 0.3 shard_map.91
  1.4 0.0 copy-start
  1.5 0.0 copy-start.1
  1.5 0.0 copy-start.5
  1.5 0.0 copy-start.6
  1.5 28.2 %all_to_all.25.r_ref = bf16[32,32,256]{2,1,0:T(8,128)(2,1)S(1)} all-to-all(bf16[32,32,256]{2,1,0:T(8,128)(2,1)S(1)} %shard_map.91), channel_id=1, replica_groups=mesh['xh'=2,'y'=8,'core'=2,'xl'=2,'z'=8] {'y','xh','core'}, dimensions={0} | all-to-all | bytes 1048576 | tf_op jit(solution)/shard_map/all_to_all | solution.py:295
  29.7 0.0 copy-start.7
  29.7 0.0 copy-start.8
  29.7 0.0 copy-done.2
  29.7 0.0 copy-done
  29.7 0.0 copy-done.1
  29.7 0.0 copy-done.5
  29.7 0.0 copy-done.6
  29.7 0.6 copy-done.7
  30.3 0.0 copy-done.8
  30.3 1.6 %shard_map.92 = (f32[1792,128]{1,0:T(8,128)S(1)}, f32[2,256,512]{2,1,0:T(8,128)S(1)}, f32[8,128]{1,0:T(8,128)S(1)}, bf16[64,128]{1,0:T(8,128)(2,1)S(1)}, f32[8,64]{1,0:T(8,128)S(1)}, /*index=5*/f32[8,128]{1,0:T(8,128)S(1)}) custom-call(bf16[32,32,256]{2,1,0:T(8,128)(2,1)S(1)} %all_to_all.25.r_ref, bf16[2,512,256]{2,1,0:T(8,128)(2,1)S(1)} %copy-done, ...), custom_call_target="tpu_custom_call" | custom-call | tf_op jit(solution)/shard_map/pallas_call | solution.py:282
  31.9 0.1 convert_element_type.15
  32.0 32.7 %all_to_all.26 = f16[128,7,2,128]{3,2,1,0:T(2,128)(2,1)S(1)} all-to-all(f16[128,7,2,128]{3,2,1,0:T(2,128)(2,1)S(1)} %bitcast.14), channel_id=1, replica_groups=mesh['xh'=2,'y'=8,'core'=2,'xl'=2,'z'=8] {'z','core','y'}, dimensions={0} | all-to-all | bytes 917504 | tf_op jit(solution)/shard_map/all_to_all | solution.py:295
  64.7 0.1 convert.2.f_ref
  64.8 0.2 shard_map.93
  65.1 7.2 %all_to_all.27 = f16[4,72,256]{2,1,0:T(8,128)(2,1)S(1)} all-to-all(f16[4,72,256]{2,1,0:T(8,128)(2,1)S(1)} %broadcast_in_dim.2), channel_id=1, replica_groups=mesh['xh'=2,'y'=8,'core'=2,'xl'=2,'z'=8] {'xl','xh'}, dimensions={0} | all-to-all | bytes 294912 | tf_op jit(solution)/shard_map/all_to_all | solution.py:295
  72.3 0.4 shard_map.94
  72.7 0.0 copy-start.3
  72.7 22.5 %all_to_all.28 = f16[128,8,128]{2,1,0:T(8,128)(2,1)S(1)} all-to-all(f16[128,8,128]{2,1,0:T(8,128)(2,1)S(1)} %convert_bitcast_fusion), channel_id=1, replica_groups=mesh['xh'=2,'y'=8,'core'=2,'xl'=2,'z'=8] {'z','core','y'}, dimensions={0} | all-to-all | bytes 524288 | tf_op jit(solution)/shard_map/all_to_all | solution.py:295
  95.3 0.0 copy-done.3
  95.3 1.9 %shard_map.95 = bf16[32,32,256]{2,1,0:T(8,128)(2,1)S(1)} custom-call(f32[1024,128]{1,0:T(8,128)S(1)} %bitcast_convert_fusion.g_ref, f32[2,256,512]{2,1,0:T(8,128)S(1)} %get-tuple-element.17.spec_ref, f32[8,128]{1,0:T(8,128)S(1)} %get-tuple-element.18.nyq_ref, f32[8,128]{1,0:T(8,128)S(1)} %get-tuple-element.19.gain_ref, ...), custom_call_target="tpu_custom_call" | custom-call | tf_op jit(solution)/shard_map/pallas_call | solution.py:282
  97.2 21.7 %all_to_all.29.r_ref = bf16[32,32,256]{2,1,0:T(8,128)(2,1)S(1)} all-to-all(bf16[32,32,256]{2,1,0:T(8,128)(2,1)S(1)} %shard_map.95), channel_id=1, replica_groups=mesh['xh'=2,'y'=8,'core'=2,'xl'=2,'z'=8] {'y','xh','core'}, dimensions={0} | all-to-all | bytes 1048576 | tf_op jit(solution)/shard_map/all_to_all | solution.py:295
  118.9 1.1 shard_map.96
  (5 shorter events, 0.1 us)
Async XLA Ops:
  0.0 29.7 %copy-start.2 = (bf16[2,2,256,512]{3,2,1,0:T(8,128)(2,1)S(1)}, bf16[2,2,256,512]{3,2,1,0:T(8,128)(2,1)}, u32[]{:S(2)}) copy-start(bf16[2,2,256,512]{3,2,1,0:T(8,128)(2,1)} %constant.10.clone.second_ref) | copy-start | bytes 3145732
  0.0 1.1 copy-start.4
  1.4 28.2 %copy-start = (bf16[2,512,256]{2,1,0:T(8,128)(2,1)S(1)}, bf16[2,512,256]{2,1,0:T(8,128)(2,1)}, u32[]{:S(2)}) copy-start(bf16[2,512,256]{2,1,0:T(8,128)(2,1)} %constant.8.clone.ends_ref) | copy-start | bytes 1572868
  1.5 28.2 %copy-start.1 = (f32[3,136,256]{2,1,0:T(8,128)S(1)}, f32[3,136,256]{2,1,0:T(8,128)}, u32[]{:S(2)}) copy-start(f32[3,136,256]{2,1,0:T(8,128)} %constant.9.clone.twf_ref) | copy-start | bytes 1253380
  1.5 28.2 %copy-start.5 = (bf16[128,64]{0,1:T(8,128)(2,1)S(1)}, bf16[128,64]{0,1:T(8,128)(2,1)}, u32[]{:S(2)}) copy-start(bf16[128,64]{0,1:T(8,128)(2,1)} %param.10) | copy-start | bytes 49156
  1.5 28.2 %copy-start.6 = (bf16[64,128]{1,0:T(8,128)(2,1)S(1)}, bf16[64,128]{1,0:T(8,128)(2,1)}, u32[]{:S(2)}) copy-start(bf16[64,128]{1,0:T(8,128)(2,1)} %cout_in_ref.1) | copy-start | bytes 49156
  29.7 0.7 copy-start.7
  29.7 0.7 copy-start.8
  72.7 22.6 %copy-start.3 = (bf16[2,2,512,256]{3,2,1,0:T(8,128)(2,1)S(1)}, bf16[2,2,512,256]{3,2,1,0:T(8,128)(2,1)}, u32[]{:S(2)}) copy-start(bf16[2,2,512,256]{3,2,1,0:T(8,128)(2,1)} %constant.11.clone.inv_ref) | copy-start | bytes 3145732

commit v8 on v7

--- a/solution.py
+++ b/solution.py
@@ -138,9 +138,8 @@
         for at, part in ((0, out_re), (RADIX, out_im)):
             high, low = split(part)
             hi[place, at : at + RADIX], lo[place, at : at + RADIX] = high, low
-            hi2[place, at : at + RADIX], lo2[place, at : at + RADIX] = high, low
         lead = im[0:8]
-        top = pl.ds(HALF * c, 16)
+        top = pl.ds(16 * c, 16)
         alt_re = jnp.concatenate(
             [jnp.where(first_row, lead * twf_ref[0, HALF:], out_re[0:8]), out_re[8:16]], 0)
         alt_im = jnp.concatenate(
@@ -164,9 +163,13 @@
         feat_ref[pl.ds(TILE + r, pieces, stride=stride), :] = jnp.broadcast_to(
             tile[r : r + 1], (pieces, 128))
     count = HALF // STEP
-    for part, (h, l) in enumerate(((hi, lo), (hi2, lo2))):
-        s = (nt(second_ref[0, part], h[...]) + nt(second_ref[0, part], l[...])
-             + nt(second_ref[1, part], h[...]))
+    for part in range(2):
+        if part:
+            for c in range(per):
+                top, place = pl.ds(16 * c, 16), pl.ds(HALF * c, 16)
+                hi[place], lo[place] = hi2[top], lo2[top]
+        s = (nt(second_ref[0, part], hi[...]) + nt(second_ref[0, part], lo[...])
+             + nt(second_ref[1, part], hi[...]))
         spec_ref[part] = s
         re, im = s[:HALF], s[HALF:]
         feature = jnp.log1p((re * re + im * im) * (1.0 / SEQ))
@@ -321,7 +324,8 @@
         [shape((pieces * (TILE + REST), HALF), f32), shape((2, RADIX, width), f32),
          shape((8, 128), f32), shape((hid, chan), bf16),
          shape((8, hid), f32), shape((8, chan), f32)],
-        [pltpu.VMEM((width, 2 * RADIX), bf16)] * 4)(
+        [pltpu.VMEM((width, 2 * RADIX), bf16)] * 2
+        + [pltpu.VMEM((16 * per, 2 * RADIX), bf16)] * 2)(
             received, t["ends"], t["twf"], t["second"],
             cond_in.T, cond_out, cond_bias.reshape(1, hid), skip_gain.reshape(1, chan))
     feat = send(feat, spread, (pieces, (TILE + REST) // 2, 2, HALF))

time: 120 us -> 120 us (level)
  no operation moved by 1% of the time
where the time goes in v8:
time: 120 us
  blocking collectives  112 us (93%)
  Pallas kernels  5.44 us (5%)
  local copies, waits for them, and re-layouts  1.81 us (2%)
    all_to_all x5, blocking collectives, exchange(): return lax.all_to_all(x, axis, split_axis=0, concat_axis=0, tiled=True)  112 us
    pallas_call x6, Pallas kernels, run(): pl.pallas_call(kernel, out_shape=outs, in_specs=[vmem] * len(args), out_s...  5.44 us

profile of v8, /device:TPU:1, one launch (start us, length us, event | category | flops | bytes accessed | tf_op | source)
XLA Modules:
  0.0 120.0 jit_solution(6397623169842558426)
XLA Ops:
  0.0 0.0 copy-start.2
  0.0 0.0 copy-start.4
  0.0 1.1 copy-done.4
  1.1 0.3 shard_map.91
  1.4 0.0 copy-start
  1.5 0.0 copy-start.1
  1.5 0.0 copy-start.5
  1.5 0.0 copy-start.6
  1.5 28.2 %all_to_all.25.r_ref = bf16[32,32,256]{2,1,0:T(8,128)(2,1)S(1)} all-to-all(bf16[32,32,256]{2,1,0:T(8,128)(2,1)S(1)} %shard_map.91), channel_id=1, replica_groups=mesh['xh'=2,'y'=8,'core'=2,'xl'=2,'z'=8] {'y','xh','core'}, dimensions={0} | all-to-all | bytes 1048576 | tf_op jit(solution)/shard_map/all_to_all | solution.py:298
  29.7 0.0 copy-start.7
  29.7 0.0 copy-start.8
  29.7 0.0 copy-done.2
  29.7 0.0 copy-done
  29.7 0.0 copy-done.1
  29.7 0.0 copy-done.5
  29.7 0.0 copy-done.6
  29.7 0.6 copy-done.7
  30.3 0.0 copy-done.8
  30.3 1.6 %shard_map.92 = (f32[1792,128]{1,0:T(8,128)S(1)}, f32[2,256,512]{2,1,0:T(8,128)S(1)}, f32[8,128]{1,0:T(8,128)S(1)}, bf16[64,128]{1,0:T(8,128)(2,1)S(1)}, f32[8,64]{1,0:T(8,128)S(1)}, /*index=5*/f32[8,128]{1,0:T(8,128)S(1)}) custom-call(bf16[32,32,256]{2,1,0:T(8,128)(2,1)S(1)} %all_to_all.25.r_ref, bf16[2,512,256]{2,1,0:T(8,128)(2,1)S(1)} %copy-done, ...), custom_call_target="tpu_custom_call" | custom-call | tf_op jit(solution)/shard_map/pallas_call | solution.py:285
  31.9 0.1 convert_element_type.15
  32.0 32.7 %all_to_all.26 = f16[128,7,2,128]{3,2,1,0:T(2,128)(2,1)S(1)} all-to-all(f16[128,7,2,128]{3,2,1,0:T(2,128)(2,1)S(1)} %bitcast.14), channel_id=1, replica_groups=mesh['xh'=2,'y'=8,'core'=2,'xl'=2,'z'=8] {'z','core','y'}, dimensions={0} | all-to-all | bytes 917504 | tf_op jit(solution)/shard_map/all_to_all | solution.py:298
  64.7 0.1 convert.2.f_ref
  64.8 0.2 shard_map.93
  65.1 7.2 %all_to_all.27 = f16[4,72,256]{2,1,0:T(8,128)(2,1)S(1)} all-to-all(f16[4,72,256]{2,1,0:T(8,128)(2,1)S(1)} %broadcast_in_dim.2), channel_id=1, replica_groups=mesh['xh'=2,'y'=8,'core'=2,'xl'=2,'z'=8] {'xl','xh'}, dimensions={0} | all-to-all | bytes 294912 | tf_op jit(solution)/shard_map/all_to_all | solution.py:298
  72.3 0.4 shard_map.94
  72.7 0.0 copy-start.3
  72.7 22.5 %all_to_all.28 = f16[128,8,128]{2,1,0:T(8,128)(2,1)S(1)} all-to-all(f16[128,8,128]{2,1,0:T(8,128)(2,1)S(1)} %convert_bitcast_fusion), channel_id=1, replica_groups=mesh['xh'=2,'y'=8,'core'=2,'xl'=2,'z'=8] {'z','core','y'}, dimensions={0} | all-to-all | bytes 524288 | tf_op jit(solution)/shard_map/all_to_all | solution.py:298
  95.3 0.0 copy-done.3
  95.3 1.9 %shard_map.95 = bf16[32,32,256]{2,1,0:T(8,128)(2,1)S(1)} custom-call(f32[1024,128]{1,0:T(8,128)S(1)} %bitcast_convert_fusion.g_ref, f32[2,256,512]{2,1,0:T(8,128)S(1)} %get-tuple-element.17.spec_ref, f32[8,128]{1,0:T(8,128)S(1)} %get-tuple-element.18.nyq_ref, f32[8,128]{1,0:T(8,128)S(1)} %get-tuple-element.19.gain_ref, ...), custom_call_target="tpu_custom_call" | custom-call | tf_op jit(solution)/shard_map/pallas_call | solution.py:285
  97.2 21.7 %all_to_all.29.r_ref = bf16[32,32,256]{2,1,0:T(8,128)(2,1)S(1)} all-to-all(bf16[32,32,256]{2,1,0:T(8,128)(2,1)S(1)} %shard_map.95), channel_id=1, replica_groups=mesh['xh'=2,'y'=8,'core'=2,'xl'=2,'z'=8] {'y','xh','core'}, dimensions={0} | all-to-all | bytes 1048576 | tf_op jit(solution)/shard_map/all_to_all | solution.py:298
  118.9 1.1 shard_map.96
  (5 shorter events, 0.1 us)
Async XLA Ops:
  0.0 29.7 %copy-start.2 = (bf16[2,2,256,512]{3,2,1,0:T(8,128)(2,1)S(1)}, bf16[2,2,256,512]{3,2,1,0:T(8,128)(2,1)}, u32[]{:S(2)}) copy-start(bf16[2,2,256,512]{3,2,1,0:T(8,128)(2,1)} %constant.10.clone.second_ref) | copy-start | bytes 3145732
  0.0 1.1 copy-start.4
  1.4 28.2 %copy-start = (bf16[2,512,256]{2,1,0:T(8,128)(2,1)S(1)}, bf16[2,512,256]{2,1,0:T(8,128)(2,1)}, u32[]{:S(2)}) copy-start(bf16[2,512,256]{2,1,0:T(8,128)(2,1)} %constant.8.clone.ends_ref) | copy-start | bytes 1572868
  1.5 28.2 %copy-start.1 = (f32[3,136,256]{2,1,0:T(8,128)S(1)}, f32[3,136,256]{2,1,0:T(8,128)}, u32[]{:S(2)}) copy-start(f32[3,136,256]{2,1,0:T(8,128)} %constant.9.clone.twf_ref) | copy-start | bytes 1253380
  1.5 28.2 %copy-start.5 = (bf16[128,64]{0,1:T(8,128)(2,1)S(1)}, bf16[128,64]{0,1:T(8,128)(2,1)}, u32[]{:S(2)}) copy-start(bf16[128,64]{0,1:T(8,128)(2,1)} %param.10) | copy-start | bytes 49156
  1.5 28.2 %copy-start.6 = (bf16[64,128]{1,0:T(8,128)(2,1)S(1)}, bf16[64,128]{1,0:T(8,128)(2,1)}, u32[]{:S(2)}) copy-start(bf16[64,128]{1,0:T(8,128)(2,1)} %cout_in_ref.1) | copy-start | bytes 49156
  29.7 0.7 copy-start.7
  29.7 0.7 copy-start.8
  72.7 22.6 %copy-start.3 = (bf16[2,2,512,256]{3,2,1,0:T(8,128)(2,1)S(1)}, bf16[2,2,512,256]{3,2,1,0:T(8,128)(2,1)}, u32[]{:S(2)}) copy-start(bf16[2,2,512,256]{3,2,1,0:T(8,128)(2,1)} %constant.11.clone.inv_ref) | copy-start | bytes 3145732

commit v9 on v7

--- a/solution.py
+++ b/solution.py
@@ -196,8 +196,8 @@
     for c in range(1, per):
         extra = extra + weights[c] * last[:, c : c + 1]
     extra = jnp.sum(extra, axis=0, keepdims=True) * (1.0 / IN_SCALE)
-    out_ref[hid:, :128] = jnp.broadcast_to(extra, (TILE, 128))
-    out_ref[hid:, 128:] = jnp.zeros((TILE, width - 128), f32)
+    out_ref[hid:, :128] = jnp.broadcast_to(extra, (STEP, 128))
+    out_ref[hid:, 128:] = jnp.zeros((STEP, width - 128), f32)
 
 
 def gelu(v):
@@ -326,11 +326,11 @@
             cond_in.T, cond_out, cond_bias.reshape(1, hid), skip_gain.reshape(1, chan))
     feat = send(feat, spread, (pieces, (TILE + REST) // 2, 2, HALF))
     partial = call(functools.partial(reduce_kernel, per, hid),
-                   shape((hid + TILE, STEP * HALF), f32))(feat)
+                   shape((hid + STEP, STEP * HALF), f32))(feat)
     partial = jnp.broadcast_to(partial[None], (groups,) + partial.shape)
-    partial = send(partial, line, partial.shape)
+    partial = send(partial, line, (groups, -1, STEP, STEP * HALF))
     gain, spare_gain = call(functools.partial(gain_kernel, per, hid),
-                            [shape((pieces * TILE, HALF), f32), shape((8, chan), f32)])(
+                            [shape((pieces * TILE, HALF), f32), shape((STEP, chan), f32)])(
                                 partial, feat, bias, cout)
     gain = send(gain, spread, (pieces, TILE, HALF))
     mixed = call(functools.partial(inverse_kernel, per, block), piece)(

time: 120 us -> 121 us (level)
  no operation moved by 1% of the time
where the time goes in v9:
time: 121 us; the launch traced here: 120 us
  blocking collectives  112 us (93%)
  Pallas kernels  5.4 us (4%)
  local copies, waits for them, and re-layouts  2.05 us (2%)
    all_to_all x5, blocking collectives, exchange(): return lax.all_to_all(x, axis, split_axis=0, concat_axis=0, tiled=True)  112 us
    pallas_call x6, Pallas kernels, run(): pl.pallas_call(kernel, out_shape=outs, in_specs=[vmem] * len(args), out_s...  5.4 us

profile of v9, /device:TPU:1, one launch (start us, length us, event | category | flops | bytes accessed | tf_op | source)
XLA Modules:
  0.0 120.2 jit_solution(2950804743374604539)
XLA Ops:
  0.0 0.0 copy-start.3
  0.0 0.0 copy-start.4
  0.0 1.1 copy-done.4
  1.1 0.3 shard_map.91
  1.4 0.0 copy-start
  1.5 0.0 copy-start.1
  1.5 0.0 copy-start.5
  1.5 0.0 copy-start.6
  1.5 28.2 %all_to_all.25.r_ref = bf16[32,32,256]{2,1,0:T(8,128)(2,1)S(1)} all-to-all(bf16[32,32,256]{2,1,0:T(8,128)(2,1)S(1)} %shard_map.91), channel_id=1, replica_groups=mesh['xh'=2,'y'=8,'core'=2,'xl'=2,'z'=8] {'y','xh','core'}, dimensions={0} | all-to-all | bytes 1048576 | tf_op jit(solution)/shard_map/all_to_all | solution.py:295
  29.7 0.0 copy-start.7
  29.7 0.0 copy-start.8
  29.7 0.0 copy-done.3
  29.7 0.0 copy-done
  29.7 0.0 copy-done.1
  29.7 0.0 copy-done.5
  29.7 0.0 copy-done.6
  29.7 0.6 copy-done.7
  30.3 0.0 copy-done.8
  30.3 1.6 %shard_map.92 = (f32[1792,128]{1,0:T(8,128)S(1)}, f32[2,256,512]{2,1,0:T(8,128)S(1)}, f32[8,128]{1,0:T(8,128)S(1)}, bf16[64,128]{1,0:T(8,128)(2,1)S(1)}, f32[8,64]{1,0:T(8,128)S(1)}, /*index=5*/f32[8,128]{1,0:T(8,128)S(1)}) custom-call(bf16[32,32,256]{2,1,0:T(8,128)(2,1)S(1)} %all_to_all.25.r_ref, bf16[2,512,256]{2,1,0:T(8,128)(2,1)S(1)} %copy-done, ...), custom_call_target="tpu_custom_call" | custom-call | tf_op jit(solution)/shard_map/pallas_call | solution.py:282
  31.9 0.1 convert_element_type.13
  32.0 32.7 %all_to_all.26 = f16[128,7,2,128]{3,2,1,0:T(2,128)(2,1)S(1)} all-to-all(f16[128,7,2,128]{3,2,1,0:T(2,128)(2,1)S(1)} %bitcast.17), channel_id=1, replica_groups=mesh['xh'=2,'y'=8,'core'=2,'xl'=2,'z'=8] {'z','core','y'}, dimensions={0} | all-to-all | bytes 917504 | tf_op jit(solution)/shard_map/all_to_all | solution.py:295
  64.7 0.1 convert.3.f_ref
  64.7 0.2 shard_map.93
  65.1 0.1 broadcast_in_dim.9
  65.1 7.2 %all_to_all.27 = f16[4,33,2,256]{3,2,1,0:T(2,128)(2,1)S(1)} all-to-all(f16[4,33,2,256]{3,2,1,0:T(2,128)(2,1)S(1)} %broadcast_in_dim.9), channel_id=1, replica_groups=mesh['xh'=2,'y'=8,'core'=2,'xl'=2,'z'=8] {'xl','xh'}, dimensions={0} | all-to-all | bytes 270336 | tf_op jit(solution)/shard_map/all_to_all | solution.py:295
  72.4 0.1 copy.13
  72.4 0.1 bitcast_convert_fusion.1
  72.5 0.1 copy.14.r_ref
  72.6 0.4 shard_map.94
  73.0 0.0 copy-start.2
  73.0 22.5 %all_to_all.28 = f16[128,8,128]{2,1,0:T(8,128)(2,1)S(1)} all-to-all(f16[128,8,128]{2,1,0:T(8,128)(2,1)S(1)} %convert_bitcast_fusion), channel_id=1, replica_groups=mesh['xh'=2,'y'=8,'core'=2,'xl'=2,'z'=8] {'z','core','y'}, dimensions={0} | all-to-all | bytes 524288 | tf_op jit(solution)/shard_map/all_to_all | solution.py:295
  95.6 0.0 copy-done.2
  95.6 1.8 %shard_map.95 = bf16[32,32,256]{2,1,0:T(8,128)(2,1)S(1)} custom-call(f32[1024,128]{1,0:T(8,128)S(1)} %bitcast_convert_fusion.g_ref, f32[2,256,512]{2,1,0:T(8,128)S(1)} %get-tuple-element.17.spec_ref, f32[8,128]{1,0:T(8,128)S(1)} %get-tuple-element.18.nyq_ref, f32[2,128]{1,0:T(2,128)S(1)} %get-tuple-element.19.gain_ref, ...), custom_call_target="tpu_custom_call" | custom-call | tf_op jit(solution)/shard_map/pallas_call | solution.py:282
  97.4 21.7 %all_to_all.29.r_ref = bf16[32,32,256]{2,1,0:T(8,128)(2,1)S(1)} all-to-all(bf16[32,32,256]{2,1,0:T(8,128)(2,1)S(1)} %shard_map.95), channel_id=1, replica_groups=mesh['xh'=2,'y'=8,'core'=2,'xl'=2,'z'=8] {'y','xh','core'}, dimensions={0} | all-to-all | bytes 1048576 | tf_op jit(solution)/shard_map/all_to_all | solution.py:295
  119.2 1.1 shard_map.96
  (4 shorter events, 0.1 us)
Async XLA Ops:
  0.0 29.7 %copy-start.3 = (bf16[2,2,256,512]{3,2,1,0:T(8,128)(2,1)S(1)}, bf16[2,2,256,512]{3,2,1,0:T(8,128)(2,1)}, u32[]{:S(2)}) copy-start(bf16[2,2,256,512]{3,2,1,0:T(8,128)(2,1)} %constant.10.clone.second_ref) | copy-start | bytes 3145732
  0.0 1.1 copy-start.4
  1.4 28.2 %copy-start = (bf16[2,512,256]{2,1,0:T(8,128)(2,1)S(1)}, bf16[2,512,256]{2,1,0:T(8,128)(2,1)}, u32[]{:S(2)}) copy-start(bf16[2,512,256]{2,1,0:T(8,128)(2,1)} %constant.8.clone.ends_ref) | copy-start | bytes 1572868
  1.5 28.2 %copy-start.1 = (f32[3,136,256]{2,1,0:T(8,128)S(1)}, f32[3,136,256]{2,1,0:T(8,128)}, u32[]{:S(2)}) copy-start(f32[3,136,256]{2,1,0:T(8,128)} %constant.9.clone.twf_ref) | copy-start | bytes 1253380
  1.5 28.2 %copy-start.5 = (bf16[128,64]{0,1:T(8,128)(2,1)S(1)}, bf16[128,64]{0,1:T(8,128)(2,1)}, u32[]{:S(2)}) copy-start(bf16[128,64]{0,1:T(8,128)(2,1)} %param.10) | copy-start | bytes 49156
  1.5 28.2 %copy-start.6 = (bf16[64,128]{1,0:T(8,128)(2,1)S(1)}, bf16[64,128]{1,0:T(8,128)(2,1)}, u32[]{:S(2)}) copy-start(bf16[64,128]{1,0:T(8,128)(2,1)} %cout_in_ref.1) | copy-start | bytes 49156
  29.7 0.7 copy-start.7
  29.7 0.7 copy-start.8
  73.0 22.6 %copy-start.2 = (bf16[2,2,512,256]{3,2,1,0:T(8,128)(2,1)S(1)}, bf16[2,2,512,256]{3,2,1,0:T(8,128)(2,1)}, u32[]{:S(2)}) copy-start(bf16[2,2,512,256]{3,2,1,0:T(8,128)(2,1)} %constant.11.clone.inv_ref) | copy-start | bytes 3145732
